TPU v7x, 1024 devices: a whole 4x4x32 slice. The times are simulated.
1024 devices in a mesh: dp: 32 (over x, z_hi, core), table: 32 (over z_lo, y).
Axes of the slice: x: 4, y: 4, z: 32 (z_hi: 4, z_lo: 8; z = z_hi * 8 + z_lo), core: 2. Of those that a mesh axis runs over, the one named last changes fastest.
Arguments:
- sparse_index: int32 [131072, 32], P(('dp', 'table')), may hold values from 0 to 34815, as said below
- frequent_rows: float32 [2048, 128], replicated, may hold values from -3 to 3
- frequent_history: float32 [2048, 128], replicated, may hold values from 0.05 to 2
- owned_rows: float32 [32768, 128], P('table'), may hold values from -3 to 3
- owned_history: float32 [32768, 128], P('table'), may hold values from 0.05 to 2
- pooled_grad: bfloat16 [131072, 1024], P(('dp', 'table')), may hold values from -0.119628906 to 0.119628906
Outputs:
- pooled: bfloat16 [131072, 1024], P(('dp', 'table'))
- updated_frequent: float32 [2048, 128], replicated
- updated_owned: float32 [32768, 128], P('table')
- history_frequent: float32 [2048, 128], replicated
- history_owned: float32 [32768, 128], P('table')
Inputs may be any that keep to these rules, and one draw needn't show every extreme that they name: `sparse_index`: infrequent row r (hybrid row 2048 + r) belongs to owner r // 1024. Among the lookups of one device (its 128 samples), at most 32 name infrequent rows of one owner; in every data group one owner receives exactly 32 from every device of the group.
All inputs are finite; a program needn't handle non-finite values.
Results may differ from a plain program's by a relative error of at most 0.013.
Values may be sent and summed in bfloat16 or wider, within the bound.
No kernel may reach another device: no remote copies, remote signals or barrier semaphores. Data moves between devices by JAX's collectives and lax.ppermute only.
A program may use at most 32 MiB of HBM per device.

v0:
```python
import jax
import jax.numpy as jnp
from jax import lax
from jax.sharding import PartitionSpec as P

E = 128
H = 4


def adagrad(weights, history, gradient):
    updated = history + gradient * gradient
    return (weights - 0.5 * gradient / jnp.sqrt(updated + 1e-08), updated)


def body(sparse_index, frequent_rows, frequent_history, owned_rows, owned_history, pooled_grad):
    owners = lax.axis_size("table")
    frequent_count = frequent_rows.shape[0]
    owned_count = owned_rows.shape[0]
    samples = sparse_index.shape[0]
    tables = pooled_grad.shape[1] // E
    flat_index = sparse_index.reshape(-1)
    lookups = flat_index.shape[0]
    capacity = lookups // (4 * owners)
    remote = flat_index >= frequent_count
    offset = jnp.where(remote, flat_index - frequent_count, 0)
    target = jnp.where(remote, offset // owned_count, owners)
    local_row = offset % owned_count
    onehot = (target[:, None] == jnp.arange(owners, dtype=jnp.int32)[None, :]).astype(jnp.int32)
    earlier = jnp.cumsum(onehot, axis=0) - onehot
    slot_rank = jnp.sum(earlier * onehot, axis=1)
    slot_index = jnp.where(remote, target * capacity + slot_rank, owners * capacity)
    requests = (
        jnp.full((owners * capacity + 1,), owned_count, jnp.int32).at[slot_index].set(local_row)
    )
    requests = requests[:-1].reshape(owners, capacity)
    lookup_grad = jnp.broadcast_to(
        pooled_grad.reshape(samples, tables, 1, E), (samples, tables, H, E)
    ).reshape(lookups, E)
    grad_slots = jnp.zeros((owners * capacity + 1, E), jnp.bfloat16).at[slot_index].set(lookup_grad)
    grad_slots = grad_slots[:-1].reshape(owners, capacity, E)
    wanted, arrived = (
        lax.all_to_all(requests, "table", split_axis=0, concat_axis=0, tiled=True),
        lax.all_to_all(grad_slots, "table", split_axis=0, concat_axis=0, tiled=True),
    )
    flat_wanted = wanted.reshape(-1)
    served = (
        owned_rows[jnp.minimum(flat_wanted, owned_count - 1)]
        .astype(jnp.bfloat16)
        .reshape(owners, capacity, E)
    )
    returned = lax.all_to_all(served, "table", split_axis=0, concat_axis=0, tiled=True)
    returned = returned.reshape(owners * capacity, E)
    remote_rows = returned[jnp.minimum(slot_index, owners * capacity - 1)]
    local_rows = frequent_rows[jnp.minimum(flat_index, frequent_count - 1)].astype(jnp.bfloat16)
    fetched = jnp.where(remote[:, None], remote_rows, local_rows)
    pooled = jnp.sum(fetched.reshape(samples, tables, H, E).astype(jnp.float32), axis=2)
    pooled = pooled.reshape(samples, tables * E).astype(jnp.bfloat16)
    frequent_slot = jnp.where(remote, frequent_count, flat_index)
    frequent_part = (
        jnp.zeros((frequent_count + 1, E), jnp.float32)
        .at[frequent_slot]
        .add(lookup_grad.astype(jnp.float32))[:-1]
    )
    owned_part = (
        jnp.zeros((owned_count + 1, E), jnp.float32)
        .at[flat_wanted]
        .add(arrived.reshape(-1, E).astype(jnp.float32))[:-1]
    )
    frequent_total = lax.psum(frequent_part, ("dp", "table"))
    owned_total = lax.psum(owned_part.astype(jnp.bfloat16), "dp").astype(jnp.float32)
    updated_frequent, history_frequent = adagrad(frequent_rows, frequent_history, frequent_total)
    updated_owned, history_owned = adagrad(owned_rows, owned_history, owned_total)
    return (pooled, updated_frequent, updated_owned, history_frequent, history_owned)


def solution(mesh):
    in_specs = (
        P(("dp", "table"), None),
        P(),
        P(),
        P("table", None),
        P("table", None),
        P(("dp", "table"), None),
    )
    out_specs = (P(("dp", "table"), None), P(), P("table", None), P(), P("table", None))
    return jax.shard_map(body, mesh=mesh, in_specs=in_specs, out_specs=out_specs, check_vma=False)
```

profile of v0, /device:TPU:1, one launch (start us, length us, event | category | flops | bytes accessed | tf_op | source)
XLA Modules:
  0.0 1532.2 jit_solution(10639214032264281009)
XLA Ops:
  8.0 0.7 broadcast_compare_fusion.1
  8.7 0.7 broadcast_add_fusion.1
  10.0 0.8 copy.13
  10.9 9.2 reduce-window.6
  20.2 0.8 slice_reduce_fusion
  21.5 0.4 fusion.8
  22.1 15.5 %scatter_custom_fusion = s32[1025]{0:T(1024)S(1)} fusion(s32[4096]{0:T(1024)S(1)} %bitcast.57, s32[4096]{0:T(1024)S(1)} %get-tuple-element.11, s32[]{:T(128)} %constant.22.clone.1), kind=kCustom, calls=%fused_computation.67 | custom fusion | bytes 4104 | tf_op jit(solution)/shard_map/scatter | solution.py:33
  37.6 0.7 all_to_all.12
  38.3 16.1 %all-to-all-start = ((s32[32,1,32]{2,1,0:T(1,128)}), s32[32,1,32]{2,1,0:T(1,128)S(1)}, u32[]{:S(2)}, u32[]{:S(2)}) async-start(s32[32,1,32]{2,1,0:T(1,128)} %all_to_all.12), calls=%async_computation | async-start | bytes 32768 | tf_op jit(solution)/shard_map/all_to_all | solution.py:42
  54.5 0.4 broadcast_in_dim.65
  54.9 10.8 scatter_custom_fusion.2
  65.7 0.7 slice.35
  66.4 12.0 all-to-all-start.2
  78.4 0.5 broadcast.381
  78.9 0.7 reduce.6
  79.8 4.1 gather_fusion
  83.8 10.0 all-to-all-done.2
  93.9 8.7 all-to-all-start.1
  102.6 22.6 %scatter_custom_fusion.1 = f32[2049,128]{1,0:T(8,128)S(1)} fusion(s32[4096]{0:T(1024)S(1)} %bitcast.59, bf16[4096,128]{1,0:T(8,128)(2,1)S(1)} %bitcast.42, f32[]{:T(128)} %constant.64.clone.1), kind=kCustom, calls=%fused_computation.7 | custom fusion | flops 1048576 | bytes 2097668 | tf_op jit(solution)/shard_map/scatter-add | solution.py:62
  125.3 1.0 slice.34
  126.4 0.3 copy.12
  126.7 0.8 copy-done
  127.6 11.0 gather_fusion.2
  138.6 881.5 %all-reduce.3.cloned.1.call-done = f32[2048,128]{1,0:T(8,128)} async-done(((f32[2048,128]{1,0:T(8,128)}), f32[2048,128]{1,0:T(8,128)}) %all-reduce.3.cloned.1.call-update) | async-done | bytes 1048592 | tf_op jit(solution)/shard_map/psum | solution.py:69
  1020.1 3.1 multiply_subtract_fusion
  1023.2 6.2 scatter_custom_fusion.3
  1029.5 0.7 slice.39
  1030.2 12.1 gather_fusion.1
  1042.4 2.1 select_reduce_fusion
  1044.5 0.8 copy.23
  1045.3 477.5 %all-reduce.5.cloned.1.call-done = bf16[1024,128]{1,0:T(8,128)(2,1)} async-done(((bf16[1024,128]{1,0:T(8,128)(2,1)}), bf16[1024,128]{1,0:T(8,128)(2,1)}) %all-reduce.5.cloned.1.call-update) | async-done | bytes 262160 | tf_op jit(solution)/shard_map/psum | solution.py:70
  1522.7 2.0 fusion.4
  (34 shorter events, 1.6 us)
Async XLA Ops:
  21.0 33.5 %copy-start.3 = (bf16[128,1024]{1,0:T(8,128)(2,1)S(1)}, bf16[128,1024]{1,0:T(8,128)(2,1)}, u32[]{:S(2)}) copy-start(bf16[128,1024]{1,0:T(8,128)(2,1)} %param.11) | copy-start | bytes 786436
  38.3 28.1 %all-to-all-start = ((s32[32,1,32]{2,1,0:T(1,128)}), s32[32,1,32]{2,1,0:T(1,128)S(1)}, u32[]{:S(2)}, u32[]{:S(2)}) async-start(s32[32,1,32]{2,1,0:T(1,128)} %all_to_all.12), calls=%async_computation | async-start | bytes 32768 | tf_op jit(solution)/shard_map/all_to_all | solution.py:42
  54.5 25.3 %copy-start.1 = (f32[1024,128]{1,0:T(8,128)S(1)}, f32[1024,128]{1,0:T(8,128)}, u32[]{:S(2)}) copy-start(f32[1024,128]{1,0:T(8,128)} %param.9) | copy-start | bytes 1572868
  66.4 27.4 %all-to-all-start.2 = ((bf16[32,32,128]{2,1,0:T(8,128)(2,1)}), bf16[32,32,128]{2,1,0:T(8,128)(2,1)S(1)}, u32[]{:S(2)}, u32[]{:S(2)}) async-start(bf16[32,32,128]{2,1,0:T(8,128)(2,1)} %bitcast.14), calls=%async_computation.2 | async-start | bytes 524288 | tf_op jit(solution)/shard_map/all_to_all | solution.py:43
  93.9 936.4 %all-to-all-start.1 = ((bf16[32,32,128]{2,1,0:T(8,128)(2,1)}), bf16[32,32,128]{2,1,0:T(8,128)(2,1)S(1)}, u32[]{:S(2)}, u32[]{:S(2)}) async-start(bf16[32,32,128]{2,1,0:T(8,128)(2,1)} %bitcast.5), calls=%async_computation.1 | async-start | bytes 524288 | tf_op jit(solution)/shard_map/all_to_all | solution.py:51
  102.6 917.5 %all-reduce.3.cloned.1.call-start = ((), (), s32[]{:S(2)}) async-start(), calls=%async_computation.3 | async-start | bytes 2097152 | tf_op jit(solution)/shard_map/psum | solution.py:69
  126.3 1.2 copy-start
  126.4 1396.4 %all-reduce.5.cloned.1.call-start = ((), (), s32[]{:S(2)}) async-start(), calls=%async_computation.4 | async-start | bytes 524288 | tf_op jit(solution)/shard_map/psum | solution.py:70
  1042.4 480.4 %copy-start.2 = (f32[1024,128]{1,0:T(8,128)S(1)}, f32[1024,128]{1,0:T(8,128)}, u32[]{:S(2)}) copy-start(f32[1024,128]{1,0:T(8,128)} %param.10) | copy-start | bytes 1572868
Sparse Core Ops, SparseCore 0:
  126.5 893.6 all-reduce.2
Sparse Core Ops, SparseCore 1:
  1030.3 492.4 all-reduce.4
where the time goes:
time: 1530 us
  waiting for transfers between devices  1370 us (90%)
  local copies, waits for them, and re-layouts  62 us (4%)
  other arithmetic  48.5 us (3%)
  starting transfers between devices  36.9 us (2%)
  between operations  15.8 us (1%)
    psum x1, waiting for transfers between devices, body(): frequent_total = lax.psum(frequent_part, ('dp', 'table'))  882 us
    psum x1, waiting for transfers between devices, body(): lax.psum(owned_part.astype(jnp.bfloat16), 'dp').astype(jnp.float32)  477 us
  transfers between devices with their start and end apart: 5, of which 3 were waited for; matrix products, arithmetic and copies ran while one was open for 5% of the time, Pallas kernels for 0%

commit v1 on v0

v1 whole, which is shorter than its diff:
```python
import functools
import jax
import jax.numpy as jnp
from jax import lax
from jax.experimental import pallas as pl
from jax.experimental.pallas import tpu as pltpu
from jax.sharding import Mesh, PartitionSpec as P

E = 128
F = 8
H = 4
B = 128
NF = 2048
RO = 1024
CAP = 32
OWNERS = 32
TAIL = 16
BLOCK = 256
MSG = CAP + TAIL
BF = jnp.bfloat16
F32 = jnp.float32
NT = (((1,), (1,)), ((), ()))
TN = (((0,), (0,)), ((), ()))


def call(kernel, outs, *args, flops=0, aliases=None):
    moved = sum(a.size * a.dtype.itemsize for a in args)
    moved += sum(o.size * o.dtype.itemsize for o in outs)
    return pl.pallas_call(
        kernel,
        out_shape=outs,
        in_specs=[pl.BlockSpec(memory_space=pltpu.VMEM)] * len(args),
        out_specs=[pl.BlockSpec(memory_space=pltpu.VMEM)] * len(outs),
        input_output_aliases=aliases or {},
        compiler_params=pltpu.CompilerParams(vmem_limit_bytes=40 * 1024 * 1024),
        cost_estimate=pl.CostEstimate(flops=flops, bytes_accessed=moved, transcendentals=0),
    )(*args)


def sds(shape, dtype):
    return jax.ShapeDtypeStruct(shape, dtype)


def onehot(positions, base):
    near = (positions - base).astype(F32).astype(BF)
    rows = lax.broadcasted_iota(jnp.int32, (BLOCK, positions.shape[1]), 0).astype(F32).astype(BF)
    total = None
    for i in range(positions.shape[0]):
        hit = jnp.where(rows == near[i : i + 1], jnp.ones((), BF), jnp.zeros((), BF))
        total = hit if total is None else total + hit
    return total


def counts(positions, base):
    return jnp.concatenate([onehot(positions[f * H : (f + 1) * H], base) for f in range(F)], axis=1)


def stack_tables(grad):
    return jnp.concatenate([grad[:, f * E : (f + 1) * E] for f in range(F)], axis=0)


def frequent_kernel(index_ref, grad_ref, part_ref):
    index = index_ref[...].T
    grad = stack_tables(grad_ref[...])
    for base in range(0, NF, BLOCK):
        part = jnp.dot(counts(index, base), grad, preferred_element_type=F32)
        part_ref[base : base + BLOCK, :] = part.astype(BF)


def slots_kernel(index_ref, grad_ref, msg_ref, req_ref, slot_ref):
    index = index_ref[...].T
    remote = index >= NF
    offset = index - NF
    owner = jnp.where(remote, offset // RO, -1)
    wanted = offset % RO + 1
    high = (wanted // 32).astype(F32)
    low = (wanted % 32).astype(F32)
    owners = lax.broadcasted_iota(jnp.int32, (OWNERS, B), 0)
    masks = [
        jnp.where(owners == owner[i : i + 1], 1.0, 0.0).astype(F32) for i in range(F * H)
    ]
    mask = jnp.concatenate(masks, axis=0).astype(BF)
    row = lax.broadcasted_iota(jnp.int32, (B, 2 * B), 0)
    col = lax.broadcasted_iota(jnp.int32, (B, 2 * B), 1)
    ones = jnp.where((col >= B) | (row < col), 1.0, 0.0).astype(BF)
    earlier = jnp.dot(mask, ones, preferred_element_type=F32)
    run = jnp.zeros((OWNERS, B), F32)
    ranks = []
    for i in range(F * H):
        before = earlier[i * OWNERS : (i + 1) * OWNERS]
        ranks.append(jnp.sum(masks[i] * (before[:, :B] + run), axis=0, keepdims=True))
        run = run + before[:, B:]
    rank = jnp.concatenate(ranks, axis=0)
    slot = jnp.where(remote, owner * CAP + rank.astype(jnp.int32), -1)
    slot_ref[...] = slot
    places = lax.broadcasted_iota(jnp.int32, (B, B), 0).astype(F32)
    what, where = [], []
    for i in range(F * H):
        what.append(
            jnp.concatenate([masks[i] * high[i : i + 1], masks[i] * low[i : i + 1]], axis=0)
        )
        where.append(jnp.where(places == rank[i : i + 1], 1.0, 0.0))
    what = jnp.concatenate(what, axis=1).astype(BF)
    where = jnp.concatenate(where, axis=1).astype(BF)
    req_ref[...] = lax.dot_general(what, where, NT, preferred_element_type=F32)
    grad = stack_tables(grad_ref[...])
    for base in range(0, OWNERS * CAP, BLOCK):
        block = jnp.dot(counts(slot, base), grad, preferred_element_type=F32)
        first = base // CAP
        last = (base + BLOCK) // CAP
        msg_ref[first:last, :CAP, :] = block.astype(BF).reshape(BLOCK // CAP, CAP, E)


def message_kernel(msg_in, req_ref, got_ref, msg_ref):
    del msg_in
    part = jnp.sum(got_ref[...].astype(F32), axis=0)
    parts = part.reshape(4, 8, 8, E)
    line = lax.broadcasted_iota(jnp.int32, (8, E), 0)
    for z in range(8):
        for y in range(4):
            t = z * 4 + y
            high = jnp.where(line == 0, req_ref[t : t + 1, :], 0.0)
            asked = jnp.where(line == 1, req_ref[OWNERS + t : OWNERS + t + 1, :], high)
            msg_ref[t, CAP:, :] = jnp.concatenate([parts[y, z], asked], axis=0).astype(BF)


def owner_kernel(got_ref, rows_ref, part_ref, served_ref, freq_ref):
    tail = got_ref[:, CAP:, :].astype(F32)
    freq_ref[...] = jnp.sum(tail[:, :8, :], axis=0)
    high = jnp.concatenate([tail[t, 8:9, :] for t in range(OWNERS)], axis=0)
    low = jnp.concatenate([tail[t, 9:10, :] for t in range(OWNERS)], axis=0)
    source = lax.broadcasted_iota(jnp.int32, (OWNERS, E), 0) % 4

    def placed(x):
        y = x
        for k in range(1, 4):
            y = jnp.where(source == k, pltpu.roll(x, CAP * k, 1), y)
        return y

    group = lax.broadcasted_iota(jnp.int32, (8, OWNERS), 0)
    member = lax.broadcasted_iota(jnp.int32, (8, OWNERS), 1) // 4
    fold = jnp.where(group == member, 1.0, 0.0).astype(BF)
    high = jnp.dot(fold, placed(high).astype(BF), preferred_element_type=F32)
    low = jnp.dot(fold, placed(low).astype(BF), preferred_element_type=F32)
    wanted = (high * 32.0 + low).astype(jnp.int32) - 1
    grads = got_ref[:, :CAP, :].reshape(OWNERS * CAP, E)
    served = jnp.zeros((OWNERS * CAP, E), F32)
    for base in range(0, RO, BLOCK):
        hits = jnp.concatenate([onehot(wanted[g : g + 1], base) for g in range(8)], axis=1)
        part = jnp.dot(hits, grads, preferred_element_type=F32)
        part_ref[base : base + BLOCK, :] = part.astype(BF)
        rows = rows_ref[base : base + BLOCK, :].astype(BF)
        served = served + lax.dot_general(hits, rows, TN, preferred_element_type=F32)
    served_ref[...] = served.astype(BF).reshape(OWNERS, CAP, E)


def slice_kernel(got_ref, freq_ref, out_ref):
    part = jnp.sum(got_ref[...].astype(F32), axis=0)
    freq = jnp.concatenate([freq_ref[...], jnp.zeros((8, E), F32)], axis=0)
    both = jnp.concatenate([part, freq], axis=0).astype(BF)
    for i in range(4):
        out_ref[i] = both


def total_kernel(got_ref, owned_ref, freq_ref):
    total = jnp.sum(got_ref[...].astype(F32), axis=0)
    owned = total[: RO // 8].astype(BF)
    for i in range(8):
        owned_ref[i] = owned
        freq_ref[i] = total[RO // 8 : RO // 8 + 8]


def spread_kernel(got_ref, out_ref):
    rows = got_ref[...].reshape(64, E).astype(BF)
    for i in range(32):
        out_ref[i] = rows


def pool_frequent_kernel(index_ref, rows_ref, out_ref):
    index = index_ref[...].T
    total = jnp.zeros((F * B, E), F32)
    for base in range(0, NF, BLOCK):
        rows = rows_ref[base : base + BLOCK, :].astype(BF)
        total = total + lax.dot_general(
            counts(index, base), rows, TN, preferred_element_type=F32
        )
    out_ref[...] = total


def pool_kernel(slot_ref, rows_ref, part_ref, out_ref):
    slot = slot_ref[...]
    total = part_ref[...]
    for base in range(0, OWNERS * CAP, BLOCK):
        rows = rows_ref[base : base + BLOCK, :]
        total = total + lax.dot_general(
            counts(slot, base), rows, TN, preferred_element_type=F32
        )
    for f in range(F):
        out_ref[:, f * E : (f + 1) * E] = total[f * B : (f + 1) * B].astype(BF)


def adagrad_kernel(rows_ref, history_ref, grad_ref, updated_ref, new_ref):
    grad = grad_ref[...].astype(F32)
    new = history_ref[...] + grad * grad
    new_ref[...] = new
    updated_ref[...] = rows_ref[...] - 0.5 * grad / jnp.sqrt(new + 1e-08)


def adagrad(rows, history, grad):
    shape = sds(rows.shape, F32)
    return call(adagrad_kernel, [shape, shape], rows, history, grad)


def swap(x, axes):
    return lax.all_to_all(x, axes, split_axis=0, concat_axis=0, tiled=True)


def body(index, frequent_rows, frequent_history, owned_rows, owned_history, grad):
    near, table = ("x", "core"), ("z_lo", "y")
    flat = F * B
    part = call(
        frequent_kernel, [sds((NF, E), BF)], index, grad, flops=2 * NF * flat * E
    )[0]
    part = swap(part.reshape(8, NF // 8, E), near)
    msg, req, slot = call(
        slots_kernel,
        [
            sds((OWNERS, MSG, E), BF),
            sds((2 * OWNERS, E), F32),
            sds((F * H, B), jnp.int32),
        ],
        index,
        grad,
        flops=2 * RO * flat * E,
    )
    msg = call(message_kernel, [sds((OWNERS, MSG, E), BF)], msg, req, part, aliases={0: 0})[0]
    got = swap(msg, table)
    owned, served, freq = call(
        owner_kernel,
        [sds((RO, E), BF), sds((OWNERS, CAP, E), BF), sds((8, E), F32)],
        got,
        owned_rows,
        flops=4 * RO * RO * E,
    )
    owned = swap(owned.reshape(8, RO // 8, E), near)
    both = call(slice_kernel, [sds((4, RO // 8 + 16, E), BF)], owned, freq)[0]
    both = swap(both, "z_hi")
    owned, freq = call(total_kernel, [sds((8, RO // 8, E), BF), sds((8, 8, E), F32)], both)
    freq = swap(freq, "z_lo")
    owned = swap(owned, near)
    freq = call(spread_kernel, [sds((32, 64, E), BF)], freq)[0]
    freq = swap(freq, ("x", "core", "y"))
    returned = swap(served, table).reshape(OWNERS * CAP, E)
    pooled = call(
        pool_frequent_kernel, [sds((flat, E), F32)], index, frequent_rows, flops=2 * NF * flat * E
    )[0]
    pooled = call(
        pool_kernel, [sds((B, F * E), BF)], slot, returned, pooled, flops=2 * RO * flat * E
    )[0]
    updated_owned, history_owned = adagrad(owned_rows, owned_history, owned.reshape(RO, E))
    updated_frequent, history_frequent = adagrad(
        frequent_rows, frequent_history, freq.reshape(NF, E)
    )
    return (pooled, updated_frequent, updated_owned, history_frequent, history_owned)


def solution(mesh):
    fine = Mesh(mesh.devices.reshape(4, 4, 2, 8, 4), ("x", "z_hi", "core", "z_lo", "y"))
    samples, table = ("x", "z_hi", "core", "z_lo", "y"), ("z_lo", "y")
    in_specs = (P(samples, None), P(), P(), P(table, None), P(table, None), P(samples, None))
    out_specs = (P(samples, None), P(), P(table, None), P(), P(table, None))
    return jax.shard_map(body, mesh=fine, in_specs=in_specs, out_specs=out_specs, check_vma=False)
```

time: 1530 us -> 191 us (0.12)
  waiting for transfers between devices: 1370 us -> 25.7 us
  blocking collectives: 0 us -> 116 us
  local copies, waits for them, and re-layouts: 62 us -> 2.19 us
  other arithmetic: 48.5 us -> 0 us
    psum x2 -> x0, waiting for transfers between devices: 1360 us -> none  [the longest x1 882 us: body(): frequent_total = lax.psum(frequent_part, ('dp', 'table'))]
    all_to_all x0 -> x5, blocking collectives: none -> 116 us  [swap(): return lax.all_to_all(x, axes, split_axis=0, concat_axis=0, tiled=True)]
    scatter-add x2 -> x0, other arithmetic: 28.8 us -> none  [the longest x1 22.6 us: body(): frequent_part = jnp.zeros((frequent_count + 1, E), jnp.float32).at[freque...]
    gather x3 -> x0, local copies, waits for them, and re-layouts: 27.2 us -> none  [the longest x1 12.1 us: body(): remote_rows = returned[jnp.minimum(slot_index, owners * capacity - 1)]]
    scatter x2 -> x0, local copies, waits for them, and re-layouts: 26.4 us -> none  [the longest x1 15.5 us: body(): jnp.full((owners * capacity + 1,), owned_count, jnp.int32).at[slot_index]]
    all_to_all x3, waiting for transfers between devices: 10 us -> 25.7 us  [swap(): return lax.all_to_all(x, axes, split_axis=0, concat_axis=0, tiled=True)]
  transfers between devices with their start and end apart: 5 -> 3, of which waited for: 3 -> 3; matrix products, arithmetic and copies ran while one was open for 5% -> 0% of each run, Pallas kernels for 0% -> 3%
where the time goes in v1:
time: 191 us; the launch traced here: 189 us
  blocking collectives  116 us (61%)
  starting transfers between devices  30.1 us (16%)
  waiting for transfers between devices  25.7 us (13%)
  Pallas kernels  14.1 us (7%)
  local copies, waits for them, and re-layouts  2.19 us (1%)
    all_to_all x5, blocking collectives, swap(): return lax.all_to_all(x, axes, split_axis=0, concat_axis=0, tiled=True)  116 us
    all_to_all x3, starting transfers between devices, swap(): return lax.all_to_all(x, axes, split_axis=0, concat_axis=0, tiled=True)  30.1 us
    all_to_all x3, waiting for transfers between devices, swap(): return lax.all_to_all(x, axes, split_axis=0, concat_axis=0, tiled=True)  25.7 us
    pallas_call x11, Pallas kernels, call(): pl.pallas_call(kernel, out_shape=outs, in_specs=[pl.BlockSpec(memory_spac...  14.1 us
  transfers between devices with their start and end apart: 3, of which 3 were waited for; matrix products, arithmetic and copies ran while one was open for 0% of the time, Pallas kernels for 3%

profile of v1, /device:TPU:1, one launch (start us, length us, event | category | flops | bytes accessed | tf_op | source)
XLA Modules:
  0.0 188.5 jit_solution(7615925107425462745)
XLA Ops:
  0.6 0.8 copy.12.index_ref
  1.4 0.0 copy-start.4
  1.5 0.9 copy-done.4
  2.4 2.8 %shard_map.102 = bf16[2048,128]{1,0:T(8,128)(2,1)} custom-call(s32[128,32]{1,0:T(8,128)S(1)} %copy.12.index_ref, bf16[128,1024]{1,0:T(8,128)(2,1)S(1)} %copy-done.4), custom_call_target="tpu_custom_call" | custom-call | flops 536870912 | bytes 802816 | tf_op jit(solution)/shard_map/pallas_call | solution.py:29
  5.2 0.0 copy-start.5
  5.2 17.7 %all-to-all-start = ((bf16[8,256,128]{2,1,0:T(8,128)(2,1)}), bf16[8,256,128]{2,1,0:T(8,128)(2,1)S(1)}, u32[]{:S(2)}, u32[]{:S(2)}) async-start(bf16[8,256,128]{2,1,0:T(8,128)(2,1)} %bitcast), calls=%async_computation | async-start | bytes 1048576 | tf_op jit(solution)/shard_map/all_to_all | solution.py:215
  22.9 0.0 copy-done.5
  22.9 1.6 shard_map.101
  24.5 7.9 %all-to-all-done.got_ref = bf16[8,256,128]{2,1,0:T(8,128)(2,1)S(1)} async-done(((bf16[8,256,128]{2,1,0:T(8,128)(2,1)}), bf16[8,256,128]{2,1,0:T(8,128)(2,1)S(1)}, u32[]{:S(2)}, u32[]{:S(2)}) %all-to-all-start) | async-done | bytes 524320 | tf_op jit(solution)/shard_map/all_to_all | solution.py:215
  32.4 0.1 shard_map.103
  32.5 0.0 copy-start.2
  32.5 23.6 %all_to_all.40.got_ref = bf16[32,48,128]{2,1,0:T(8,128)(2,1)S(1)} all-to-all(bf16[32,48,128]{2,1,0:T(8,128)(2,1)S(1)} %shard_map.103), channel_id=1, replica_groups=mesh['x'=4,'z_hi'=4,'core'=2,'z_lo'=8,'y'=4] {'z_lo','y'}, dimensions={0} | all-to-all | bytes 786432 | tf_op jit(solution)/shard_map/all_to_all | solution.py:215
  56.1 0.0 copy-done.2
  56.1 2.2 %shard_map.104 = (bf16[1024,128]{1,0:T(8,128)(2,1)S(1)}, bf16[32,32,128]{2,1,0:T(8,128)(2,1)}, f32[8,128]{1,0:T(8,128)S(1)}) custom-call(bf16[32,48,128]{2,1,0:T(8,128)(2,1)S(1)} %all_to_all.40.got_ref, f32[1024,128]{1,0:T(8,128)S(1)} %copy-done.2), custom_call_target="tpu_custom_call" | custom-call | flops 536870912 | bytes 1445888 | tf_op jit(solution)/shard_map/pallas_call | solution.py:29
  58.2 14.0 %all_to_all.41.got_ref = bf16[8,128,128]{2,1,0:T(8,128)(2,1)S(1)} all-to-all(bf16[8,128,128]{2,1,0:T(8,128)(2,1)S(1)} %bitcast.8), channel_id=1, replica_groups=mesh['x'=4,'z_hi'=4,'core'=2,'z_lo'=8,'y'=4] {'x','core'}, dimensions={0} | all-to-all | bytes 524288 | tf_op jit(solution)/shard_map/all_to_all | solution.py:215
  72.3 43.0 %all_to_all.42.got_ref = bf16[4,144,128]{2,1,0:T(8,128)(2,1)S(1)} all-to-all(bf16[4,144,128]{2,1,0:T(8,128)(2,1)S(1)} %shard_map.107), channel_id=1, replica_groups=mesh['x'=4,'z_hi'=4,'core'=2,'z_lo'=8,'y'=4] {'z_hi'}, dimensions={0} | all-to-all | bytes 294912 | tf_op jit(solution)/shard_map/all_to_all | solution.py:215
  115.3 0.7 shard_map.108
  116.0 18.5 %all_to_all.43.got_ref = f32[8,8,128]{2,1,0:T(8,128)S(1)} all-to-all(f32[8,8,128]{2,1,0:T(8,128)S(1)} %get-tuple-element.23), channel_id=1, replica_groups=mesh['x'=4,'z_hi'=4,'core'=2,'z_lo'=8,'y'=4] {'z_lo'}, dimensions={0} | all-to-all | bytes 65536 | tf_op jit(solution)/shard_map/all_to_all | solution.py:215
  134.5 8.5 %all-to-all-start.7 = ((bf16[8,128,128]{2,1,0:T(8,128)(2,1)}), bf16[8,128,128]{2,1,0:T(8,128)(2,1)S(1)}, u32[]{:S(2)}, u32[]{:S(2)}) async-start(bf16[8,128,128]{2,1,0:T(8,128)(2,1)} %get-tuple-element.25), calls=%async_computation.7 | async-start | bytes 524288 | tf_op jit(solution)/shard_map/all_to_all | solution.py:215
  143.2 6.5 %all-to-all-done.7 = bf16[8,128,128]{2,1,0:T(8,128)(2,1)S(1)} async-done(((bf16[8,128,128]{2,1,0:T(8,128)(2,1)}), bf16[8,128,128]{2,1,0:T(8,128)(2,1)S(1)}, u32[]{:S(2)}, u32[]{:S(2)}) %all-to-all-start.7) | async-done | bytes 262176 | tf_op jit(solution)/shard_map/all_to_all | solution.py:215
  149.6 16.6 %all_to_all.44 = bf16[32,64,128]{2,1,0:T(8,128)(2,1)S(1)} all-to-all(bf16[32,64,128]{2,1,0:T(8,128)(2,1)S(1)} %shard_map.109), channel_id=1, replica_groups=mesh['x'=4,'z_hi'=4,'core'=2,'z_lo'=8,'y'=4] {'x','core','y'}, dimensions={0} | all-to-all | bytes 1048576 | tf_op jit(solution)/shard_map/all_to_all | solution.py:215
  166.2 3.9 %all-to-all-start.2 = ((bf16[32,32,128]{2,1,0:T(8,128)(2,1)}), bf16[32,32,128]{2,1,0:T(8,128)(2,1)S(1)}, u32[]{:S(2)}, u32[]{:S(2)}) async-start(bf16[32,32,128]{2,1,0:T(8,128)(2,1)} %get-tuple-element.20), calls=%async_computation.2 | async-start | bytes 524288 | tf_op jit(solution)/shard_map/all_to_all | solution.py:215
  170.1 0.0 copy-done
  170.1 0.0 copy-start.3
  170.1 2.0 %shard_map.105.part_ref = f32[1024,128]{1,0:T(8,128)S(1)} custom-call(s32[128,32]{1,0:T(8,128)S(1)} %copy.12.index_ref, f32[2048,128]{1,0:T(8,128)S(1)} %copy-done), custom_call_target="tpu_custom_call" | custom-call | flops 536870912 | bytes 1589248 | tf_op jit(solution)/shard_map/pallas_call | solution.py:29
  172.1 0.0 copy-start.1
  172.1 0.0 copy-done.3
  172.1 1.2 shard_map.111
  173.3 0.4 copy-done.1
  173.7 1.7 shard_map.110
  175.5 11.4 %all-to-all-done.2 = bf16[32,32,128]{2,1,0:T(8,128)(2,1)S(1)} async-done(((bf16[32,32,128]{2,1,0:T(8,128)(2,1)}), bf16[32,32,128]{2,1,0:T(8,128)(2,1)S(1)}, u32[]{:S(2)}, u32[]{:S(2)}) %all-to-all-start.2) | async-done | bytes 262176 | tf_op jit(solution)/shard_map/all_to_all | solution.py:215
  186.8 1.7 shard_map.106
  (3 shorter events, 0.1 us)
Async XLA Ops:
  1.4 1.0 copy-start.4
  5.2 17.7 %copy-start.5 = (bf16[128,1024]{1,0:T(8,128)(2,1)S(1)}, bf16[128,1024]{1,0:T(8,128)(2,1)}, u32[]{:S(2)}) copy-start(bf16[128,1024]{1,0:T(8,128)(2,1)} %grad_ref.3) | copy-start | bytes 786436
  5.2 27.2 %all-to-all-start = ((bf16[8,256,128]{2,1,0:T(8,128)(2,1)}), bf16[8,256,128]{2,1,0:T(8,128)(2,1)S(1)}, u32[]{:S(2)}, u32[]{:S(2)}) async-start(bf16[8,256,128]{2,1,0:T(8,128)(2,1)} %bitcast), calls=%async_computation | async-start | bytes 1048576 | tf_op jit(solution)/shard_map/all_to_all | solution.py:215
  32.5 23.6 %copy-start.2 = (f32[1024,128]{1,0:T(8,128)S(1)}, f32[1024,128]{1,0:T(8,128)}, u32[]{:S(2)}) copy-start(f32[1024,128]{1,0:T(8,128)} %rows_ref.7) | copy-start | bytes 1572868
  134.5 15.1 %all-to-all-start.7 = ((bf16[8,128,128]{2,1,0:T(8,128)(2,1)}), bf16[8,128,128]{2,1,0:T(8,128)(2,1)S(1)}, u32[]{:S(2)}, u32[]{:S(2)}) async-start(bf16[8,128,128]{2,1,0:T(8,128)(2,1)} %get-tuple-element.25), calls=%async_computation.7 | async-start | bytes 524288 | tf_op jit(solution)/shard_map/all_to_all | solution.py:215
  143.1 27.0 %copy-start = (f32[2048,128]{1,0:T(8,128)S(1)}, f32[2048,128]{1,0:T(8,128)}, u32[]{:S(2)}) copy-start(f32[2048,128]{1,0:T(8,128)} %rows_ref.6) | copy-start | bytes 3145732
  166.2 20.6 %all-to-all-start.2 = ((bf16[32,32,128]{2,1,0:T(8,128)(2,1)}), bf16[32,32,128]{2,1,0:T(8,128)(2,1)S(1)}, u32[]{:S(2)}, u32[]{:S(2)}) async-start(bf16[32,32,128]{2,1,0:T(8,128)(2,1)} %get-tuple-element.20), calls=%async_computation.2 | async-start | bytes 524288 | tf_op jit(solution)/shard_map/all_to_all | solution.py:215
  170.1 2.0 %copy-start.3 = (f32[1024,128]{1,0:T(8,128)S(1)}, f32[1024,128]{1,0:T(8,128)}, u32[]{:S(2)}) copy-start(f32[1024,128]{1,0:T(8,128)} %history_ref.3) | copy-start | bytes 1572868
  172.1 1.6 copy-start.1

commit v2 on v1

--- a/solution.py
+++ b/solution.py
@@ -162,17 +162,18 @@
         out_ref[i] = both
 
 
-def total_kernel(got_ref, owned_ref, freq_ref):
+def total_kernel(got_ref, served_ref, msg_ref, owned_ref):
     total = jnp.sum(got_ref[...].astype(F32), axis=0)
-    owned = total[: RO // 8].astype(BF)
+    owned_ref[...] = total[: RO // 8].astype(BF)
+    freq = total[RO // 8 : RO // 8 + 8].astype(BF)
+    for t in range(OWNERS):
+        msg_ref[t] = jnp.concatenate([served_ref[t], freq], axis=0)
+
+
+def spread_kernel(got_ref, owned_ref, out_ref):
+    freq = [got_ref[z * 4 + y].astype(F32)[CAP:] for y in range(4) for z in range(8)]
+    rows = jnp.concatenate([jnp.concatenate(freq, axis=0).astype(BF), owned_ref[...]], axis=0)
     for i in range(8):
-        owned_ref[i] = owned
-        freq_ref[i] = total[RO // 8 : RO // 8 + 8]
-
-
-def spread_kernel(got_ref, out_ref):
-    rows = got_ref[...].reshape(64, E).astype(BF)
-    for i in range(32):
         out_ref[i] = rows
 
 
@@ -191,7 +192,7 @@
     slot = slot_ref[...]
     total = part_ref[...]
     for base in range(0, OWNERS * CAP, BLOCK):
-        rows = rows_ref[base : base + BLOCK, :]
+        rows = rows_ref[base // CAP : (base + BLOCK) // CAP, :CAP, :].reshape(BLOCK, E)
         total = total + lax.dot_general(
             counts(slot, base), rows, TN, preferred_element_type=F32
         )
@@ -199,16 +200,26 @@
         out_ref[:, f * E : (f + 1) * E] = total[f * B : (f + 1) * B].astype(BF)
 
 
-def adagrad_kernel(rows_ref, history_ref, grad_ref, updated_ref, new_ref):
-    grad = grad_ref[...].astype(F32)
-    new = history_ref[...] + grad * grad
-    new_ref[...] = new
-    updated_ref[...] = rows_ref[...] - 0.5 * grad / jnp.sqrt(new + 1e-08)
-
-
 def adagrad(rows, history, grad):
-    shape = sds(rows.shape, F32)
-    return call(adagrad_kernel, [shape, shape], rows, history, grad)
+    grad = grad.astype(F32)
+    new = history + grad * grad
+    return rows - 0.5 * grad / jnp.sqrt(new + 1e-08), new
+
+
+def adagrad_kernel(
+    got_ref, rows_ref, history_ref, owned_ref, owned_history_ref,
+    updated_ref, new_ref, updated_owned_ref, new_owned_ref,
+):
+    part = NF // 8
+    for i in range(8):
+        at = pl.ds(i * part, part)
+        updated_ref[at, :], new_ref[at, :] = adagrad(
+            rows_ref[at, :], history_ref[at, :], got_ref[i, :part, :]
+        )
+        at = pl.ds(i * (RO // 8), RO // 8)
+        updated_owned_ref[at, :], new_owned_ref[at, :] = adagrad(
+            owned_ref[at, :], owned_history_ref[at, :], got_ref[i, part:, :]
+        )
 
 
 def swap(x, axes):
@@ -245,21 +256,26 @@
     owned = swap(owned.reshape(8, RO // 8, E), near)
     both = call(slice_kernel, [sds((4, RO // 8 + 16, E), BF)], owned, freq)[0]
     both = swap(both, "z_hi")
-    owned, freq = call(total_kernel, [sds((8, RO // 8, E), BF), sds((8, 8, E), F32)], both)
-    freq = swap(freq, "z_lo")
-    owned = swap(owned, near)
-    freq = call(spread_kernel, [sds((32, 64, E), BF)], freq)[0]
-    freq = swap(freq, ("x", "core", "y"))
-    returned = swap(served, table).reshape(OWNERS * CAP, E)
+    msg, owned = call(
+        total_kernel, [sds((OWNERS, CAP + 8, E), BF), sds((RO // 8, E), BF)], both, served
+    )
+    got = swap(msg, table)
+    both = call(spread_kernel, [sds((8, (NF + RO) // 8, E), BF)], got, owned)[0]
+    both = swap(both, near)
     pooled = call(
         pool_frequent_kernel, [sds((flat, E), F32)], index, frequent_rows, flops=2 * NF * flat * E
     )[0]
     pooled = call(
-        pool_kernel, [sds((B, F * E), BF)], slot, returned, pooled, flops=2 * RO * flat * E
+        pool_kernel, [sds((B, F * E), BF)], slot, got, pooled, flops=2 * RO * flat * E
     )[0]
-    updated_owned, history_owned = adagrad(owned_rows, owned_history, owned.reshape(RO, E))
-    updated_frequent, history_frequent = adagrad(
-        frequent_rows, frequent_history, freq.reshape(NF, E)
+    updated_frequent, history_frequent, updated_owned, history_owned = call(
+        adagrad_kernel,
+        [sds((NF, E), F32), sds((NF, E), F32), sds((RO, E), F32), sds((RO, E), F32)],
+        both,
+        frequent_rows,
+        frequent_history,
+        owned_rows,
+        owned_history,
     )
     return (pooled, updated_frequent, updated_owned, history_frequent, history_owned)
 

time: 191 us -> 169 us (0.88); the launches traced: 189 us -> 169 us
  blocking collectives: 116 us -> 105 us
  waiting for transfers between devices: 25.7 us -> 16.5 us
    all_to_all x5 -> x4, blocking collectives: 116 us -> 105 us  [swap(): return lax.all_to_all(x, axes, split_axis=0, concat_axis=0, tiled=True)]
    all_to_all x3 -> x2, waiting for transfers between devices: 25.7 us -> 16.5 us  [swap(): return lax.all_to_all(x, axes, split_axis=0, concat_axis=0, tiled=True)]
    unnamed x13 -> x15, local copies, waits for them, and re-layouts: 2.19 us -> 3.86 us
    pallas_call x11 -> x10, Pallas kernels: 14.1 us -> 13.1 us  [call(): pl.pallas_call(kernel, out_shape=outs, in_specs=[pl.BlockSpec(memory_spac...]
    all_to_all x3 -> x2, starting transfers between devices: 30.1 us -> 29.2 us  [swap(): return lax.all_to_all(x, axes, split_axis=0, concat_axis=0, tiled=True)]
  transfers between devices with their start and end apart: 3 -> 2, of which waited for: 3 -> 2; matrix products, arithmetic and copies ran while one was open for 0% -> 0% of each run, Pallas kernels for 3% -> 3%
where the time goes in v2:
time: 169 us
  blocking collectives  105 us (62%)
  starting transfers between devices  29.2 us (17%)
  waiting for transfers between devices  16.5 us (10%)
  Pallas kernels  13.1 us (8%)
  local copies, waits for them, and re-layouts  3.86 us (2%)
    all_to_all x4, blocking collectives, swap(): return lax.all_to_all(x, axes, split_axis=0, concat_axis=0, tiled=True)  105 us
    all_to_all x2, starting transfers between devices, swap(): return lax.all_to_all(x, axes, split_axis=0, concat_axis=0, tiled=True)  29.2 us
    all_to_all x2, waiting for transfers between devices, swap(): return lax.all_to_all(x, axes, split_axis=0, concat_axis=0, tiled=True)  16.5 us
    pallas_call x10, Pallas kernels, call(): pl.pallas_call(kernel, out_shape=outs, in_specs=[pl.BlockSpec(memory_spac...  13.1 us
    unnamed x15, local copies, waits for them, and re-layouts  3.86 us
  transfers between devices with their start and end apart: 2, of which 2 were waited for; matrix products, arithmetic and copies ran while one was open for 0% of the time, Pallas kernels for 3%

profile of v2, /device:TPU:1, one launch (start us, length us, event | category | flops | bytes accessed | tf_op | source)
XLA Modules:
  0.0 168.8 jit_solution(17450772758020244600)
XLA Ops:
  0.6 0.8 copy.12.index_ref
  1.4 0.0 copy-start.5
  1.5 0.9 copy-done.5
  2.4 2.8 %shard_map.102 = bf16[2048,128]{1,0:T(8,128)(2,1)} custom-call(s32[128,32]{1,0:T(8,128)S(1)} %copy.12.index_ref, bf16[128,1024]{1,0:T(8,128)(2,1)S(1)} %copy-done.5), custom_call_target="tpu_custom_call" | custom-call | flops 536870912 | bytes 802816 | tf_op jit(solution)/shard_map/pallas_call | solution.py:29
  5.2 0.0 copy-start.6
  5.2 17.7 %all-to-all-start = ((bf16[8,256,128]{2,1,0:T(8,128)(2,1)}), bf16[8,256,128]{2,1,0:T(8,128)(2,1)S(1)}, u32[]{:S(2)}, u32[]{:S(2)}) async-start(bf16[8,256,128]{2,1,0:T(8,128)(2,1)} %bitcast), calls=%async_computation | async-start | bytes 1048576 | tf_op jit(solution)/shard_map/all_to_all | solution.py:226
  22.9 0.0 copy-done.6
  22.9 1.6 shard_map.101
  24.5 7.9 %all-to-all-done.got_ref = bf16[8,256,128]{2,1,0:T(8,128)(2,1)S(1)} async-done(((bf16[8,256,128]{2,1,0:T(8,128)(2,1)}), bf16[8,256,128]{2,1,0:T(8,128)(2,1)S(1)}, u32[]{:S(2)}, u32[]{:S(2)}) %all-to-all-start) | async-done | bytes 524320 | tf_op jit(solution)/shard_map/all_to_all | solution.py:226
  32.4 0.1 shard_map.103
  32.5 0.0 copy-start.2
  32.5 23.6 %all_to_all.30.got_ref = bf16[32,48,128]{2,1,0:T(8,128)(2,1)S(1)} all-to-all(bf16[32,48,128]{2,1,0:T(8,128)(2,1)S(1)} %shard_map.103), channel_id=1, replica_groups=mesh['x'=4,'z_hi'=4,'core'=2,'z_lo'=8,'y'=4] {'z_lo','y'}, dimensions={0} | all-to-all | bytes 786432 | tf_op jit(solution)/shard_map/all_to_all | solution.py:226
  56.1 0.0 copy-done.2
  56.1 1.5 shard_map.104
  57.5 14.0 %all_to_all.31.got_ref = bf16[8,128,128]{2,1,0:T(8,128)(2,1)S(1)} all-to-all(bf16[8,128,128]{2,1,0:T(8,128)(2,1)S(1)} %bitcast.2), channel_id=1, replica_groups=mesh['x'=4,'z_hi'=4,'core'=2,'z_lo'=8,'y'=4] {'x','core'}, dimensions={0} | all-to-all | bytes 524288 | tf_op jit(solution)/shard_map/all_to_all | solution.py:226
  71.6 43.0 %all_to_all.32.got_ref = bf16[4,144,128]{2,1,0:T(8,128)(2,1)S(1)} all-to-all(bf16[4,144,128]{2,1,0:T(8,128)(2,1)S(1)} %shard_map.105), channel_id=1, replica_groups=mesh['x'=4,'z_hi'=4,'core'=2,'z_lo'=8,'y'=4] {'z_hi'}, dimensions={0} | all-to-all | bytes 294912 | tf_op jit(solution)/shard_map/all_to_all | solution.py:226
  114.6 0.1 shard_map.106
  114.7 24.9 %all_to_all.33.rows_ref.got_ref = bf16[32,40,128]{2,1,0:T(8,128)(2,1)S(1)} all-to-all(bf16[32,40,128]{2,1,0:T(8,128)(2,1)S(1)} %get-tuple-element.23), channel_id=1, replica_groups=mesh['x'=4,'z_hi'=4,'core'=2,'z_lo'=8,'y'=4] {'z_lo','y'}, dimensions={0} | all-to-all | bytes 655360 | tf_op jit(solution)/shard_map/all_to_all | solution.py:226
  139.6 1.0 shard_map.109
  140.5 0.0 copy-start
  140.5 11.5 %all-to-all-start.5 = ((bf16[8,384,128]{2,1,0:T(8,128)(2,1)}), bf16[8,384,128]{2,1,0:T(8,128)(2,1)S(1)}, u32[]{:S(2)}, u32[]{:S(2)}) async-start(bf16[8,384,128]{2,1,0:T(8,128)(2,1)} %shard_map.109), calls=%async_computation.5 | async-start | bytes 1572864 | tf_op jit(solution)/shard_map/all_to_all | solution.py:226
  152.1 0.0 copy-done
  152.1 2.0 %shard_map.107.part_ref = f32[1024,128]{1,0:T(8,128)S(1)} custom-call(s32[128,32]{1,0:T(8,128)S(1)} %copy.12.index_ref, f32[2048,128]{1,0:T(8,128)S(1)} %copy-done), custom_call_target="tpu_custom_call" | custom-call | flops 536870912 | bytes 1589248 | tf_op jit(solution)/shard_map/pallas_call | solution.py:29
  154.1 0.0 copy-start.1
  154.1 1.7 %shard_map.108 = bf16[128,1024]{1,0:T(8,128)(2,1)} custom-call(s32[32,128]{1,0:T(8,128)S(1)} %get-tuple-element.17.slot_ref, bf16[32,40,128]{2,1,0:T(8,128)(2,1)S(1)} %all_to_all.33.rows_ref.got_ref, f32[1024,128]{1,0:T(8,128)S(1)} %shard_map.107.part_ref), custom_call_target="tpu_custom_call" | custom-call | flops 268435456 | bytes 1130496 | tf_op jit(solution)/shard_map/pallas_call | solution.py:29
  155.8 8.6 %all-to-all-done.5.got_ref = bf16[8,384,128]{2,1,0:T(8,128)(2,1)S(1)} async-done(((bf16[8,384,128]{2,1,0:T(8,128)(2,1)}), bf16[8,384,128]{2,1,0:T(8,128)(2,1)S(1)}, u32[]{:S(2)}, u32[]{:S(2)}) %all-to-all-start.5) | async-done | bytes 786464 | tf_op jit(solution)/shard_map/all_to_all | solution.py:226
  164.4 0.0 copy-done.1
  164.4 0.0 copy-start.3
  164.4 1.0 copy-done.3
  165.4 0.0 copy-start.4
  165.4 1.0 copy-done.4
  166.5 2.3 %shard_map.110 = (f32[2048,128]{1,0:T(8,128)}, f32[2048,128]{1,0:T(8,128)}, f32[1024,128]{1,0:T(8,128)}, f32[1024,128]{1,0:T(8,128)}) custom-call(bf16[8,384,128]{2,1,0:T(8,128)(2,1)S(1)} %all-to-all-done.5.got_ref, f32[2048,128]{1,0:T(8,128)S(1)} %copy-done, f32[2048,128]{1,0:T(8,128)S(1)} %copy-done.1, f32[1024,128]{1,0:T(8,128)S(1)} %copy-done.3, ...), custom_call_target="tpu_custom_call" | custom-call | bytes 7077888 | tf_op jit(solution)/shard_map/pallas_call | solution.py:29
  (1 shorter events, 0.0 us)
Async XLA Ops:
  1.4 1.0 copy-start.5
  5.2 17.7 %copy-start.6 = (bf16[128,1024]{1,0:T(8,128)(2,1)S(1)}, bf16[128,1024]{1,0:T(8,128)(2,1)}, u32[]{:S(2)}) copy-start(bf16[128,1024]{1,0:T(8,128)(2,1)} %grad_ref.3) | copy-start | bytes 786436
  5.2 27.2 %all-to-all-start = ((bf16[8,256,128]{2,1,0:T(8,128)(2,1)}), bf16[8,256,128]{2,1,0:T(8,128)(2,1)S(1)}, u32[]{:S(2)}, u32[]{:S(2)}) async-start(bf16[8,256,128]{2,1,0:T(8,128)(2,1)} %bitcast), calls=%async_computation | async-start | bytes 1048576 | tf_op jit(solution)/shard_map/all_to_all | solution.py:226
  32.5 23.6 %copy-start.2 = (f32[1024,128]{1,0:T(8,128)S(1)}, f32[1024,128]{1,0:T(8,128)}, u32[]{:S(2)}) copy-start(f32[1024,128]{1,0:T(8,128)} %owned_ref.1) | copy-start | bytes 1572868
  140.5 11.5 %copy-start = (f32[2048,128]{1,0:T(8,128)S(1)}, f32[2048,128]{1,0:T(8,128)}, u32[]{:S(2)}) copy-start(f32[2048,128]{1,0:T(8,128)} %rows_ref.5) | copy-start | bytes 3145732
  140.5 23.8 %all-to-all-start.5 = ((bf16[8,384,128]{2,1,0:T(8,128)(2,1)}), bf16[8,384,128]{2,1,0:T(8,128)(2,1)S(1)}, u32[]{:S(2)}, u32[]{:S(2)}) async-start(bf16[8,384,128]{2,1,0:T(8,128)(2,1)} %shard_map.109), calls=%async_computation.5 | async-start | bytes 1572864 | tf_op jit(solution)/shard_map/all_to_all | solution.py:226
  154.1 10.3 %copy-start.1 = (f32[2048,128]{1,0:T(8,128)S(1)}, f32[2048,128]{1,0:T(8,128)}, u32[]{:S(2)}) copy-start(f32[2048,128]{1,0:T(8,128)} %history_ref.1) | copy-start | bytes 3145732
  164.4 1.0 copy-start.3
  165.4 1.0 copy-start.4

commit v3 on v2

--- a/solution.py
+++ b/solution.py
@@ -158,12 +158,15 @@
     part = jnp.sum(got_ref[...].astype(F32), axis=0)
     freq = jnp.concatenate([freq_ref[...], jnp.zeros((8, E), F32)], axis=0)
     both = jnp.concatenate([part, freq], axis=0).astype(BF)
-    for i in range(4):
-        out_ref[i] = both
-
-
-def total_kernel(got_ref, served_ref, msg_ref, owned_ref):
-    total = jnp.sum(got_ref[...].astype(F32), axis=0)
+    out_ref[0] = both
+
+
+def pair_kernel(a_ref, b_ref, out_ref):
+    out_ref[...] = (a_ref[...].astype(F32) + b_ref[...].astype(F32)).astype(BF)
+
+
+def total_kernel(mine_ref, got_ref, served_ref, msg_ref, owned_ref):
+    total = mine_ref[...].astype(F32) + got_ref[...].astype(F32)
     owned_ref[...] = total[: RO // 8].astype(BF)
     freq = total[RO // 8 : RO // 8 + 8].astype(BF)
     for t in range(OWNERS):
@@ -254,10 +257,13 @@
         flops=4 * RO * RO * E,
     )
     owned = swap(owned.reshape(8, RO // 8, E), near)
-    both = call(slice_kernel, [sds((4, RO // 8 + 16, E), BF)], owned, freq)[0]
-    both = swap(both, "z_hi")
+    both = call(slice_kernel, [sds((1, RO // 8 + 16, E), BF)], owned, freq)[0]
+    both = both[0]
+    got = lax.ppermute(both, "z_hi", [(0, 1), (1, 0), (2, 3), (3, 2)])
+    both = call(pair_kernel, [sds((RO // 8 + 16, E), BF)], both, got)[0]
+    got = lax.ppermute(both, "z_hi", [(1, 2), (2, 1), (3, 0), (0, 3)])
     msg, owned = call(
-        total_kernel, [sds((OWNERS, CAP + 8, E), BF), sds((RO // 8, E), BF)], both, served
+        total_kernel, [sds((OWNERS, CAP + 8, E), BF), sds((RO // 8, E), BF)], both, got, served
     )
     got = swap(msg, table)
     both = call(spread_kernel, [sds((8, (NF + RO) // 8, E), BF)], got, owned)[0]

time: 169 us -> 156 us (0.923)
  blocking collectives: 105 us -> 58.8 us
  starting transfers between devices: 29.2 us -> 47.1 us
  waiting for transfers between devices: 16.5 us -> 31.4 us
    all_to_all x4 -> x3, blocking collectives: 105 us -> 58.8 us  [swap(): return lax.all_to_all(x, axes, split_axis=0, concat_axis=0, tiled=True)]
    ppermute x0 -> x2, starting transfers between devices: none -> 21.3 us  [the longest x1 15.4 us: body(): got = lax.ppermute(both, 'z_hi', [(0, 1), (1, 0), (2, 3), (3, 2)])]
    ppermute x0 -> x2, waiting for transfers between devices: none -> 14.9 us  [the longest x1 7.54 us: body(): got = lax.ppermute(both, 'z_hi', [(1, 2), (2, 1), (3, 0), (0, 3)])]
    all_to_all x2, starting transfers between devices: 29.2 us -> 25.8 us  [swap(): return lax.all_to_all(x, axes, split_axis=0, concat_axis=0, tiled=True)]
    pallas_call x10 -> x11, Pallas kernels: 13.1 us -> 13.1 us  [call(): pl.pallas_call(kernel, out_shape=outs, in_specs=[pl.BlockSpec(memory_spac...]
  transfers between devices with their start and end apart: 2 -> 4, of which waited for: 2 -> 4; matrix products, arithmetic and copies ran while one was open for 0% -> 0% of each run, Pallas kernels for 3% -> 3%
where the time goes in v3:
time: 156 us; the launch traced here: 155 us
  blocking collectives  58.8 us (38%)
  starting transfers between devices  47.1 us (30%)
  waiting for transfers between devices  31.4 us (20%)
  Pallas kernels  13.1 us (8%)
  local copies, waits for them, and re-layouts  3.86 us (2%)
    all_to_all x3, blocking collectives, swap(): return lax.all_to_all(x, axes, split_axis=0, concat_axis=0, tiled=True)  58.8 us
    all_to_all x2, starting transfers between devices, swap(): return lax.all_to_all(x, axes, split_axis=0, concat_axis=0, tiled=True)  25.8 us
    all_to_all x2, waiting for transfers between devices, swap(): return lax.all_to_all(x, axes, split_axis=0, concat_axis=0, tiled=True)  16.5 us
    ppermute x1, starting transfers between devices, body(): got = lax.ppermute(both, 'z_hi', [(0, 1), (1, 0), (2, 3), (3, 2)])  15.4 us
    pallas_call x11, Pallas kernels, call(): pl.pallas_call(kernel, out_shape=outs, in_specs=[pl.BlockSpec(memory_spac...  13.1 us
    ppermute x1, waiting for transfers between devices, body(): got = lax.ppermute(both, 'z_hi', [(1, 2), (2, 1), (3, 0), (0, 3)])  7.54 us
    ppermute x1, waiting for transfers between devices, body(): got = lax.ppermute(both, 'z_hi', [(0, 1), (1, 0), (2, 3), (3, 2)])  7.35 us
    ppermute x1, starting transfers between devices, body(): got = lax.ppermute(both, 'z_hi', [(1, 2), (2, 1), (3, 0), (0, 3)])  5.86 us
  transfers between devices with their start and end apart: 4, of which 4 were waited for; matrix products, arithmetic and copies ran while one was open for 0% of the time, Pallas kernels for 3%

profile of v3, /device:TPU:1, one launch (start us, length us, event | category | flops | bytes accessed | tf_op | source)
XLA Modules:
  0.0 154.9 jit_solution(7490890917741692198)
XLA Ops:
  0.6 0.8 copy.12.index_ref
  1.4 0.0 copy-start.5
  1.5 0.9 copy-done.5
  2.4 2.8 %shard_map.102 = bf16[2048,128]{1,0:T(8,128)(2,1)} custom-call(s32[128,32]{1,0:T(8,128)S(1)} %copy.12.index_ref, bf16[128,1024]{1,0:T(8,128)(2,1)S(1)} %copy-done.5), custom_call_target="tpu_custom_call" | custom-call | flops 536870912 | bytes 802816 | tf_op jit(solution)/shard_map/pallas_call | solution.py:29
  5.2 0.0 copy-start.6
  5.2 17.7 %all-to-all-start = ((bf16[8,256,128]{2,1,0:T(8,128)(2,1)}), bf16[8,256,128]{2,1,0:T(8,128)(2,1)S(1)}, u32[]{:S(2)}, u32[]{:S(2)}) async-start(bf16[8,256,128]{2,1,0:T(8,128)(2,1)} %bitcast), calls=%async_computation | async-start | bytes 1048576 | tf_op jit(solution)/shard_map/all_to_all | solution.py:229
  22.9 0.0 copy-done.6
  22.9 1.6 %shard_map.101 = (bf16[32,48,128]{2,1,0:T(8,128)(2,1)S(1)}, f32[64,128]{1,0:T(8,128)S(1)}, s32[32,128]{1,0:T(8,128)S(1)}) custom-call(s32[128,32]{1,0:T(8,128)S(1)} %copy.12.index_ref, bf16[128,1024]{1,0:T(8,128)(2,1)S(1)} %copy-done.6), custom_call_target="tpu_custom_call" | custom-call | flops 268435456 | bytes 720896 | tf_op jit(solution)/shard_map/pallas_call | solution.py:29
  24.5 7.9 %all-to-all-done.got_ref = bf16[8,256,128]{2,1,0:T(8,128)(2,1)S(1)} async-done(((bf16[8,256,128]{2,1,0:T(8,128)(2,1)}), bf16[8,256,128]{2,1,0:T(8,128)(2,1)S(1)}, u32[]{:S(2)}, u32[]{:S(2)}) %all-to-all-start) | async-done | bytes 524320 | tf_op jit(solution)/shard_map/all_to_all | solution.py:229
  32.4 0.1 shard_map.103
  32.5 0.0 copy-start.2
  32.5 23.6 %all_to_all.25.got_ref = bf16[32,48,128]{2,1,0:T(8,128)(2,1)S(1)} all-to-all(bf16[32,48,128]{2,1,0:T(8,128)(2,1)S(1)} %shard_map.103), channel_id=1, replica_groups=mesh['x'=4,'z_hi'=4,'core'=2,'z_lo'=8,'y'=4] {'z_lo','y'}, dimensions={0} | all-to-all | bytes 786432 | tf_op jit(solution)/shard_map/all_to_all | solution.py:229
  56.1 0.0 copy-done.2
  56.1 1.5 shard_map.104
  57.5 14.0 %all_to_all.26.got_ref = bf16[8,128,128]{2,1,0:T(8,128)(2,1)S(1)} all-to-all(bf16[8,128,128]{2,1,0:T(8,128)(2,1)S(1)} %bitcast.3), channel_id=1, replica_groups=mesh['x'=4,'z_hi'=4,'core'=2,'z_lo'=8,'y'=4] {'x','core'}, dimensions={0} | all-to-all | bytes 524288 | tf_op jit(solution)/shard_map/all_to_all | solution.py:229
  71.6 15.4 %collective-permute-start = (bf16[144,128]{1,0:T(8,128)(2,1)S(1)}, bf16[144,128]{1,0:T(8,128)(2,1)S(1)}, u32[]{:S(2)}, u32[]{:S(2)}) collective-permute-start(bf16[144,128]{1,0:T(8,128)(2,1)S(1)} %bitcast.4), channel_id=1, source_target_pairs={{0,64},{64,0},{128,192},{192,128},{1,65},{65,1},{129,193},{193,129... | collective-permute-start | bytes 110600 | tf_op jit(solution)/shard_map/ppermute | solution.py:262
  87.0 7.3 %collective-permute-done.b_ref = bf16[144,128]{1,0:T(8,128)(2,1)S(1)} collective-permute-done((bf16[144,128]{1,0:T(8,128)(2,1)S(1)}, bf16[144,128]{1,0:T(8,128)(2,1)S(1)}, u32[]{:S(2)}, u32[]{:S(2)}) %collective-permute-start) | collective-permute-done | bytes 36896 | tf_op jit(solution)/shard_map/ppermute | solution.py:262
  94.4 5.9 %collective-permute-start.1 = (bf16[144,128]{1,0:T(8,128)(2,1)S(1)}, bf16[144,128]{1,0:T(8,128)(2,1)S(1)}, u32[]{:S(2)}, u32[]{:S(2)}) collective-permute-start(bf16[144,128]{1,0:T(8,128)(2,1)S(1)} %shard_map.106.mine_ref), channel_id=1, source_target_pairs={{64,128},{128,64},{192,0},{0,192},{65,129},{129,65},{193,1},{1,193... | collective-permute-start | bytes 110600 | tf_op jit(solution)/shard_map/ppermute | solution.py:264
  100.3 7.5 %collective-permute-done.1.got_ref = bf16[144,128]{1,0:T(8,128)(2,1)S(1)} collective-permute-done((bf16[144,128]{1,0:T(8,128)(2,1)S(1)}, bf16[144,128]{1,0:T(8,128)(2,1)S(1)}, u32[]{:S(2)}, u32[]{:S(2)}) %collective-permute-start.1) | collective-permute-done | bytes 36896 | tf_op jit(solution)/shard_map/ppermute | solution.py:264
  107.8 0.1 shard_map.107
  107.9 21.3 %all_to_all.27.rows_ref.got_ref = bf16[32,40,128]{2,1,0:T(8,128)(2,1)S(1)} all-to-all(bf16[32,40,128]{2,1,0:T(8,128)(2,1)S(1)} %get-tuple-element.23), channel_id=1, replica_groups=mesh['x'=4,'z_hi'=4,'core'=2,'z_lo'=8,'y'=4] {'z_lo','y'}, dimensions={0} | all-to-all | bytes 655360 | tf_op jit(solution)/shard_map/all_to_all | solution.py:229
  129.1 1.0 shard_map.110
  130.1 8.1 %all-to-all-start.4 = ((bf16[8,384,128]{2,1,0:T(8,128)(2,1)}), bf16[8,384,128]{2,1,0:T(8,128)(2,1)S(1)}, u32[]{:S(2)}, u32[]{:S(2)}) async-start(bf16[8,384,128]{2,1,0:T(8,128)(2,1)} %shard_map.110), calls=%async_computation.4 | async-start | bytes 1572864 | tf_op jit(solution)/shard_map/all_to_all | solution.py:229
  138.2 0.0 copy-done
  138.2 2.0 %shard_map.108.part_ref = f32[1024,128]{1,0:T(8,128)S(1)} custom-call(s32[128,32]{1,0:T(8,128)S(1)} %copy.12.index_ref, f32[2048,128]{1,0:T(8,128)S(1)} %copy-done), custom_call_target="tpu_custom_call" | custom-call | flops 536870912 | bytes 1589248 | tf_op jit(solution)/shard_map/pallas_call | solution.py:29
  140.2 0.0 copy-start.1
  140.2 1.7 %shard_map.109 = bf16[128,1024]{1,0:T(8,128)(2,1)} custom-call(s32[32,128]{1,0:T(8,128)S(1)} %get-tuple-element.17.slot_ref, bf16[32,40,128]{2,1,0:T(8,128)(2,1)S(1)} %all_to_all.27.rows_ref.got_ref, f32[1024,128]{1,0:T(8,128)S(1)} %shard_map.108.part_ref), custom_call_target="tpu_custom_call" | custom-call | flops 268435456 | bytes 1130496 | tf_op jit(solution)/shard_map/pallas_call | solution.py:29
  141.9 8.6 %all-to-all-done.4.got_ref = bf16[8,384,128]{2,1,0:T(8,128)(2,1)S(1)} async-done(((bf16[8,384,128]{2,1,0:T(8,128)(2,1)}), bf16[8,384,128]{2,1,0:T(8,128)(2,1)S(1)}, u32[]{:S(2)}, u32[]{:S(2)}) %all-to-all-start.4) | async-done | bytes 786464 | tf_op jit(solution)/shard_map/all_to_all | solution.py:229
  150.5 0.0 copy-done.1
  150.5 1.0 copy-done.3
  151.5 1.0 copy-done.4
  152.6 2.3 %shard_map.111 = (f32[2048,128]{1,0:T(8,128)}, f32[2048,128]{1,0:T(8,128)}, f32[1024,128]{1,0:T(8,128)}, f32[1024,128]{1,0:T(8,128)}) custom-call(bf16[8,384,128]{2,1,0:T(8,128)(2,1)S(1)} %all-to-all-done.4.got_ref, f32[2048,128]{1,0:T(8,128)S(1)} %copy-done, f32[2048,128]{1,0:T(8,128)S(1)} %copy-done.1, f32[1024,128]{1,0:T(8,128)S(1)} %copy-done.3, ...), custom_call_target="tpu_custom_call" | custom-call | bytes 7077888 | tf_op jit(solution)/shard_map/pallas_call | solution.py:29
  (5 shorter events, 0.1 us)
Async XLA Ops:
  1.4 1.0 copy-start.5
  5.2 17.7 %copy-start.6 = (bf16[128,1024]{1,0:T(8,128)(2,1)S(1)}, bf16[128,1024]{1,0:T(8,128)(2,1)}, u32[]{:S(2)}) copy-start(bf16[128,1024]{1,0:T(8,128)(2,1)} %grad_ref.3) | copy-start | bytes 786436
  5.2 27.2 %all-to-all-start = ((bf16[8,256,128]{2,1,0:T(8,128)(2,1)}), bf16[8,256,128]{2,1,0:T(8,128)(2,1)S(1)}, u32[]{:S(2)}, u32[]{:S(2)}) async-start(bf16[8,256,128]{2,1,0:T(8,128)(2,1)} %bitcast), calls=%async_computation | async-start | bytes 1048576 | tf_op jit(solution)/shard_map/all_to_all | solution.py:229
  32.5 23.6 %copy-start.2 = (f32[1024,128]{1,0:T(8,128)S(1)}, f32[1024,128]{1,0:T(8,128)}, u32[]{:S(2)}) copy-start(f32[1024,128]{1,0:T(8,128)} %owned_ref.1) | copy-start | bytes 1572868
  71.6 22.8 %collective-permute-start = (bf16[144,128]{1,0:T(8,128)(2,1)S(1)}, bf16[144,128]{1,0:T(8,128)(2,1)S(1)}, u32[]{:S(2)}, u32[]{:S(2)}) collective-permute-start(bf16[144,128]{1,0:T(8,128)(2,1)S(1)} %bitcast.4), channel_id=1, source_target_pairs={{0,64},{64,0},{128,192},{192,128},{1,65},{65,1},{129,193},{193,129... | collective-permute-start | bytes 110600 | tf_op jit(solution)/shard_map/ppermute | solution.py:262
  94.4 13.4 %collective-permute-start.1 = (bf16[144,128]{1,0:T(8,128)(2,1)S(1)}, bf16[144,128]{1,0:T(8,128)(2,1)S(1)}, u32[]{:S(2)}, u32[]{:S(2)}) collective-permute-start(bf16[144,128]{1,0:T(8,128)(2,1)S(1)} %shard_map.106.mine_ref), channel_id=1, source_target_pairs={{64,128},{128,64},{192,0},{0,192},{65,129},{129,65},{193,1},{1,193... | collective-permute-start | bytes 110600 | tf_op jit(solution)/shard_map/ppermute | solution.py:264
  130.1 8.1 %copy-start = (f32[2048,128]{1,0:T(8,128)S(1)}, f32[2048,128]{1,0:T(8,128)}, u32[]{:S(2)}) copy-start(f32[2048,128]{1,0:T(8,128)} %rows_ref.5) | copy-start | bytes 3145732
  130.1 20.4 %all-to-all-start.4 = ((bf16[8,384,128]{2,1,0:T(8,128)(2,1)}), bf16[8,384,128]{2,1,0:T(8,128)(2,1)S(1)}, u32[]{:S(2)}, u32[]{:S(2)}) async-start(bf16[8,384,128]{2,1,0:T(8,128)(2,1)} %shard_map.110), calls=%async_computation.4 | async-start | bytes 1572864 | tf_op jit(solution)/shard_map/all_to_all | solution.py:229
  140.2 10.3 %copy-start.1 = (f32[2048,128]{1,0:T(8,128)S(1)}, f32[2048,128]{1,0:T(8,128)}, u32[]{:S(2)}) copy-start(f32[2048,128]{1,0:T(8,128)} %history_ref.1) | copy-start | bytes 3145732
  150.5 1.0 copy-start.3
  151.5 1.0 copy-start.4

commit v4 on v1

--- a/solution.py
+++ b/solution.py
@@ -14,25 +14,28 @@
 RO = 1024
 CAP = 32
 OWNERS = 32
-TAIL = 16
 BLOCK = 256
-MSG = CAP + TAIL
+QUARTER = NF // 128
+MSG = CAP + QUARTER + 2
+PAIR_COST = 10**12
 BF = jnp.bfloat16
 F32 = jnp.float32
 NT = (((1,), (1,)), ((), ()))
 TN = (((0,), (0,)), ((), ()))
 
 
-def call(kernel, outs, *args, flops=0, aliases=None):
+def call(kernel, outs, *args, flops=0, vmem=40):
     moved = sum(a.size * a.dtype.itemsize for a in args)
     moved += sum(o.size * o.dtype.itemsize for o in outs)
     return pl.pallas_call(
         kernel,
         out_shape=outs,
-        in_specs=[pl.BlockSpec(memory_space=pltpu.VMEM)] * len(args),
+        in_specs=[
+            pl.BlockSpec(memory_space=pltpu.SMEM if len(a.shape) == 1 else pltpu.VMEM)
+            for a in args
+        ],
         out_specs=[pl.BlockSpec(memory_space=pltpu.VMEM)] * len(outs),
-        input_output_aliases=aliases or {},
-        compiler_params=pltpu.CompilerParams(vmem_limit_bytes=40 * 1024 * 1024),
+        compiler_params=pltpu.CompilerParams(vmem_limit_bytes=vmem * 1024 * 1024),
         cost_estimate=pl.CostEstimate(flops=flops, bytes_accessed=moved, transcendentals=0),
     )(*args)
 
@@ -67,7 +70,7 @@
         part_ref[base : base + BLOCK, :] = part.astype(BF)
 
 
-def slots_kernel(index_ref, grad_ref, msg_ref, req_ref, slot_ref):
+def slots_kernel(index_ref, grad_ref, out_ref, req_ref, slot_ref):
     index = index_ref[...].T
     remote = index >= NF
     offset = index - NF
@@ -108,27 +111,29 @@
         block = jnp.dot(counts(slot, base), grad, preferred_element_type=F32)
         first = base // CAP
         last = (base + BLOCK) // CAP
-        msg_ref[first:last, :CAP, :] = block.astype(BF).reshape(BLOCK // CAP, CAP, E)
-
-
-def message_kernel(msg_in, req_ref, got_ref, msg_ref):
-    del msg_in
+        out_ref[first:last] = block.astype(BF).reshape(BLOCK // CAP, CAP, E)
+
+
+def message_kernel(slots_ref, req_ref, got_ref, msg_ref):
     part = jnp.sum(got_ref[...].astype(F32), axis=0)
-    parts = part.reshape(4, 8, 8, E)
-    line = lax.broadcasted_iota(jnp.int32, (8, E), 0)
-    for z in range(8):
-        for y in range(4):
-            t = z * 4 + y
-            high = jnp.where(line == 0, req_ref[t : t + 1, :], 0.0)
-            asked = jnp.where(line == 1, req_ref[OWNERS + t : OWNERS + t + 1, :], high)
-            msg_ref[t, CAP:, :] = jnp.concatenate([parts[y, z], asked], axis=0).astype(BF)
-
-
-def owner_kernel(got_ref, rows_ref, part_ref, served_ref, freq_ref):
-    tail = got_ref[:, CAP:, :].astype(F32)
-    freq_ref[...] = jnp.sum(tail[:, :8, :], axis=0)
-    high = jnp.concatenate([tail[t, 8:9, :] for t in range(OWNERS)], axis=0)
-    low = jnp.concatenate([tail[t, 9:10, :] for t in range(OWNERS)], axis=0)
+    for t in range(OWNERS):
+        row = t % 4 * QUARTER
+        high = req_ref[t : t + 1, :]
+        low = req_ref[OWNERS + t : OWNERS + t + 1, :]
+        tail = jnp.concatenate([part[row : row + QUARTER], high, low], axis=0).astype(BF)
+        msg_ref[t] = jnp.concatenate([slots_ref[t], tail], axis=0)
+
+
+def hits_of(wanted, base):
+    return jnp.concatenate([onehot(wanted[g : g + 1], base) for g in range(8)], axis=1)
+
+
+def owner_kernel(got_ref, part_ref, wanted_ref, freq_ref):
+    tails = [got_ref[t].astype(F32)[CAP:] for t in range(OWNERS)]
+    quarters = [sum(t[:QUARTER] for t in tails[y::4]) for y in range(4)]
+    freq_ref[...] = jnp.concatenate(quarters, axis=0).astype(BF)
+    high = jnp.concatenate([t[QUARTER : QUARTER + 1] for t in tails], axis=0)
+    low = jnp.concatenate([t[QUARTER + 1 :] for t in tails], axis=0)
     source = lax.broadcasted_iota(jnp.int32, (OWNERS, E), 0) % 4
 
     def placed(x):
@@ -143,36 +148,48 @@
     high = jnp.dot(fold, placed(high).astype(BF), preferred_element_type=F32)
     low = jnp.dot(fold, placed(low).astype(BF), preferred_element_type=F32)
     wanted = (high * 32.0 + low).astype(jnp.int32) - 1
-    grads = got_ref[:, :CAP, :].reshape(OWNERS * CAP, E)
+    wanted_ref[...] = wanted
+    grads = jnp.concatenate([got_ref[t][:CAP] for t in range(OWNERS)], axis=0)
+    for base in range(0, RO, BLOCK):
+        part = jnp.dot(hits_of(wanted, base), grads, preferred_element_type=F32)
+        part_ref[base : base + BLOCK, :] = part.astype(BF)
+
+
+def serve_kernel(wanted_ref, rows_ref, after_ref, out_ref):
+    del after_ref
+    wanted = wanted_ref[...]
     served = jnp.zeros((OWNERS * CAP, E), F32)
     for base in range(0, RO, BLOCK):
-        hits = jnp.concatenate([onehot(wanted[g : g + 1], base) for g in range(8)], axis=1)
-        part = jnp.dot(hits, grads, preferred_element_type=F32)
-        part_ref[base : base + BLOCK, :] = part.astype(BF)
         rows = rows_ref[base : base + BLOCK, :].astype(BF)
-        served = served + lax.dot_general(hits, rows, TN, preferred_element_type=F32)
-    served_ref[...] = served.astype(BF).reshape(OWNERS, CAP, E)
+        served = served + lax.dot_general(
+            hits_of(wanted, base), rows, TN, preferred_element_type=F32
+        )
+    out_ref[...] = served.astype(BF).reshape(OWNERS, CAP, E)
 
 
 def slice_kernel(got_ref, freq_ref, out_ref):
-    part = jnp.sum(got_ref[...].astype(F32), axis=0)
-    freq = jnp.concatenate([freq_ref[...], jnp.zeros((8, E), F32)], axis=0)
-    both = jnp.concatenate([part, freq], axis=0).astype(BF)
+    out_ref[: RO // 8, :] = jnp.sum(got_ref[...].astype(F32), axis=0).astype(BF)
+    out_ref[RO // 8 :, :] = freq_ref[...]
+
+
+def pair_kernel(a_ref, b_ref, out_ref):
+    out_ref[...] = (a_ref[...].astype(F32) + b_ref[...].astype(F32)).astype(BF)
+
+
+def total_kernel(mine_ref, got_ref, after_ref, owned_ref, freq_ref):
+    del after_ref
+    total = (mine_ref[...].astype(F32) + got_ref[...].astype(F32)).astype(BF)
+    owned_ref[...] = total[: RO // 8]
     for i in range(4):
-        out_ref[i] = both
-
-
-def total_kernel(got_ref, owned_ref, freq_ref):
-    total = jnp.sum(got_ref[...].astype(F32), axis=0)
-    owned = total[: RO // 8].astype(BF)
-    for i in range(8):
-        owned_ref[i] = owned
-        freq_ref[i] = total[RO // 8 : RO // 8 + 8]
-
-
-def spread_kernel(got_ref, out_ref):
-    rows = got_ref[...].reshape(64, E).astype(BF)
-    for i in range(32):
+        freq_ref[i] = total[RO // 8 :]
+
+
+def spread_kernel(got_ref, owned_ref, out_ref):
+    freq = [
+        got_ref[q, y * QUARTER : (y + 1) * QUARTER, :] for y in range(4) for q in range(4)
+    ]
+    rows = jnp.concatenate(freq + [owned_ref[...]], axis=0)
+    for i in range(4):
         out_ref[i] = rows
 
 
@@ -199,33 +216,85 @@
         out_ref[:, f * E : (f + 1) * E] = total[f * B : (f + 1) * B].astype(BF)
 
 
-def adagrad_kernel(rows_ref, history_ref, grad_ref, updated_ref, new_ref):
-    grad = grad_ref[...].astype(F32)
-    new = history_ref[...] + grad * grad
-    new_ref[...] = new
-    updated_ref[...] = rows_ref[...] - 0.5 * grad / jnp.sqrt(new + 1e-08)
-
-
 def adagrad(rows, history, grad):
-    shape = sds(rows.shape, F32)
-    return call(adagrad_kernel, [shape, shape], rows, history, grad)
+    grad = grad.astype(F32)
+    new = history + grad * grad
+    return rows - 0.5 * grad / jnp.sqrt(new + 1e-08), new
+
+
+def adagrad_kernel(core_ref, mine_ref, other_ref, rows_ref, history_ref, updated_ref, new_ref):
+    core = core_ref[0]
+    part = updated_ref.shape[0] // 8
+    first = mine_ref.shape[1] - part if part == RO // 8 else 0
+    for got_ref, c in ((mine_ref, core), (other_ref, 1 - core)):
+        for i in range(4):
+            at = pl.ds(pl.multiple_of((2 * i + c) * part, part), part)
+            updated_ref[at, :], new_ref[at, :] = adagrad(
+                rows_ref[at, :], history_ref[at, :], got_ref[i, first : first + part, :]
+            )
 
 
 def swap(x, axes):
     return lax.all_to_all(x, axes, split_axis=0, concat_axis=0, tiled=True)
 
 
+def window(z_hi, core, z_lo):
+    return (z_hi - (core == 1 and z_lo < 4)) % 4
+
+
+def z_hi_of(w, core, z_lo):
+    return [z for z in range(4) if window(z, core, z_lo) == w][0]
+
+
+def owner_groups():
+    return [
+        [
+            ((z_hi_of(w, core, z) * 2 + core) * 8 + z) * 4 + y
+            for z in range(8)
+            for y in range(4)
+        ]
+        for core in range(2)
+        for w in range(4)
+    ]
+
+
+def far_pairs(step):
+    pairs = []
+    for core in range(2):
+        for w in range(4):
+            other = w ^ 1 if core == step else (3 - w) % 4
+            for z in range(8):
+                a, b = z_hi_of(w, core, z), z_hi_of(other, core, z)
+                pairs.append(((a * 2 + core) * 8 + z, (b * 2 + core) * 8 + z))
+    return pairs
+
+
+def far(x, step):
+    return lax.ppermute(x, ("z_hi", "core", "z_lo"), far_pairs(step))
+
+
+def to_owners(x):
+    return lax.all_to_all(
+        x,
+        ("z_hi", "core", "z_lo", "y"),
+        split_axis=0,
+        concat_axis=0,
+        tiled=True,
+        axis_index_groups=owner_groups(),
+    )
+
+
 def body(index, frequent_rows, frequent_history, owned_rows, owned_history, grad):
-    near, table = ("x", "core"), ("z_lo", "y")
+    near, plane = ("x", "core"), ("x", "core", "y")
     flat = F * B
     part = call(
         frequent_kernel, [sds((NF, E), BF)], index, grad, flops=2 * NF * flat * E
     )[0]
-    part = swap(part.reshape(8, NF // 8, E), near)
-    msg, req, slot = call(
+    part = swap(part.reshape(32, NF // 32, E), plane)
+    slots, req, slot = call(
         slots_kernel,
         [
-            sds((OWNERS, MSG, E), BF),
+            sds((OWNERS, CAP, E), BF),
             sds((2 * OWNERS, E), F32),
             sds((F * H, B), jnp.int32),
         ],
@@ -233,33 +302,53 @@
         grad,
         flops=2 * RO * flat * E,
     )
-    msg = call(message_kernel, [sds((OWNERS, MSG, E), BF)], msg, req, part, aliases={0: 0})[0]
-    got = swap(msg, table)
-    owned, served, freq = call(
+    msg = call(message_kernel, [sds((OWNERS, MSG, E), BF)], slots, req, part)[0]
+    got = to_owners(msg)
+    owned, wanted, freq = call(
         owner_kernel,
-        [sds((RO, E), BF), sds((OWNERS, CAP, E), BF), sds((8, E), F32)],
+        [sds((RO, E), BF), sds((8, E), jnp.int32), sds((NF // 32, E), BF)],
         got,
+        flops=2 * RO * RO * E,
+    )
+    owned = swap(owned.reshape(8, RO // 8, E), near)
+    both = call(slice_kernel, [sds((RO // 8 + NF // 32, E), BF)], owned, freq)[0]
+    served = call(
+        serve_kernel,
+        [sds((OWNERS, CAP, E), BF)],
+        wanted,
         owned_rows,
-        flops=4 * RO * RO * E,
-    )
-    owned = swap(owned.reshape(8, RO // 8, E), near)
-    both = call(slice_kernel, [sds((4, RO // 8 + 16, E), BF)], owned, freq)[0]
-    both = swap(both, "z_hi")
-    owned, freq = call(total_kernel, [sds((8, RO // 8, E), BF), sds((8, 8, E), F32)], both)
-    freq = swap(freq, "z_lo")
-    owned = swap(owned, near)
-    freq = call(spread_kernel, [sds((32, 64, E), BF)], freq)[0]
-    freq = swap(freq, ("x", "core", "y"))
-    returned = swap(served, table).reshape(OWNERS * CAP, E)
+        both,
+        flops=2 * RO * RO * E,
+    )[0]
+    returned = to_owners(served)
+    got = far(both, 0)
+    both = call(pair_kernel, [sds(both.shape, BF)], both, got, flops=PAIR_COST)[0]
+    got = far(both, 1)
+    got, returned = lax.optimization_barrier((got, returned))
     pooled = call(
         pool_frequent_kernel, [sds((flat, E), F32)], index, frequent_rows, flops=2 * NF * flat * E
     )[0]
+    owned, freq = call(
+        total_kernel, [sds((RO // 8, E), BF), sds((4, NF // 32, E), BF)], both, got, pooled
+    )
+    freq = swap(freq, "y")
+    both = call(spread_kernel, [sds((4, (NF + RO) // 8, E), BF)], freq, owned)[0]
+    mine = swap(both, "x")
+    other = lax.ppermute(mine, "core", [(0, 1), (1, 0)])
     pooled = call(
-        pool_kernel, [sds((B, F * E), BF)], slot, returned, pooled, flops=2 * RO * flat * E
+        pool_kernel,
+        [sds((B, F * E), BF)],
+        slot,
+        returned.reshape(OWNERS * CAP, E),
+        pooled,
+        flops=2 * RO * flat * E,
     )[0]
-    updated_owned, history_owned = adagrad(owned_rows, owned_history, owned.reshape(RO, E))
-    updated_frequent, history_frequent = adagrad(
-        frequent_rows, frequent_history, freq.reshape(NF, E)
+    core = lax.axis_index("core").reshape(1)
+    updated_frequent, history_frequent = call(
+        adagrad_kernel, [sds((NF, E), F32)] * 2, core, mine, other, frequent_rows, frequent_history
+    )
+    updated_owned, history_owned = call(
+        adagrad_kernel, [sds((RO, E), F32)] * 2, core, mine, other, owned_rows, owned_history
     )
     return (pooled, updated_frequent, updated_owned, history_frequent, history_owned)
 

time: 191 us -> 140 us (0.73)
  blocking collectives: 116 us -> 56.5 us
  starting transfers between devices: 30.1 us -> 49.5 us
  waiting for transfers between devices: 25.7 us -> 14.8 us
    all_to_all x5 -> x3, blocking collectives: 116 us -> 26 us  [swap(): return lax.all_to_all(x, axes, split_axis=0, concat_axis=0, tiled=True)]
    all_to_all x0 -> x1, blocking collectives: none -> 30.5 us  [to_owners(): lax.all_to_all(x, ('z_hi', 'core', 'z_lo', 'y'), split_axis=0, concat_axi...]
    ppermute x0 -> x3, starting transfers between devices: none -> 27 us  [the longest x2 18.9 us: far(): return lax.ppermute(x, ('z_hi', 'core', 'z_lo'), far_pairs(step))]
    all_to_all x3 -> x1, waiting for transfers between devices: 25.7 us -> 9.51 us  [swap(): return lax.all_to_all(x, axes, split_axis=0, concat_axis=0, tiled=True)]
    all_to_all x3 -> x1, starting transfers between devices: 30.1 us -> 17.8 us  [swap(): return lax.all_to_all(x, axes, split_axis=0, concat_axis=0, tiled=True)]
    ppermute x0 -> x3, waiting for transfers between devices: none -> 5.3 us  [the longest x2 5.3 us: far(): return lax.ppermute(x, ('z_hi', 'core', 'z_lo'), far_pairs(step))]
    all_to_all x0 -> x1, starting transfers between devices: none -> 4.6 us  [to_owners(): lax.all_to_all(x, ('z_hi', 'core', 'z_lo', 'y'), split_axis=0, concat_axi...]
    pallas_call x11 -> x13, Pallas kernels: 14.1 us -> 14.8 us  [call(): pl.pallas_call(kernel, out_shape=outs, in_specs=[pl.BlockSpec(memory_spac...]
  transfers between devices with their start and end apart: 3 -> 5, of which waited for: 3 -> 2; matrix products, arithmetic and copies ran while one was open for 0% -> 0% of each run, Pallas kernels for 3% -> 6%
where the time goes in v4:
time: 140 us; the launch traced here: 138 us
  blocking collectives  56.5 us (40%)
  starting transfers between devices  49.5 us (35%)
  Pallas kernels  14.8 us (11%)
  waiting for transfers between devices  14.8 us (11%)
  local copies, waits for them, and re-layouts  1.8 us (1%)
    all_to_all x1, blocking collectives, to_owners(): lax.all_to_all(x, ('z_hi', 'core', 'z_lo', 'y'), split_axis=0, concat_axi...  30.5 us
    all_to_all x3, blocking collectives, swap(): return lax.all_to_all(x, axes, split_axis=0, concat_axis=0, tiled=True)  26 us
    ppermute x2, starting transfers between devices, far(): return lax.ppermute(x, ('z_hi', 'core', 'z_lo'), far_pairs(step))  18.9 us
    all_to_all x1, starting transfers between devices, swap(): return lax.all_to_all(x, axes, split_axis=0, concat_axis=0, tiled=True)  17.8 us
    pallas_call x13, Pallas kernels, call(): pl.pallas_call(kernel, out_shape=outs, in_specs=[pl.BlockSpec(memory_spac...  14.8 us
    all_to_all x1, waiting for transfers between devices, swap(): return lax.all_to_all(x, axes, split_axis=0, concat_axis=0, tiled=True)  9.51 us
    ppermute x1, starting transfers between devices, body(): other = lax.ppermute(mine, 'core', [(0, 1), (1, 0)])  8.12 us
    ppermute x2, waiting for transfers between devices, far(): return lax.ppermute(x, ('z_hi', 'core', 'z_lo'), far_pairs(step))  5.3 us
  transfers between devices with their start and end apart: 5, of which 2 were waited for; matrix products, arithmetic and copies ran while one was open for 0% of the time, Pallas kernels for 6%

profile of v4, /device:TPU:1, one launch (start us, length us, event | category | flops | bytes accessed | tf_op | source)
XLA Modules:
  0.0 138.2 jit_solution(2794502479253202293)
XLA Ops:
  0.6 0.8 copy.11.index_ref
  1.4 0.0 copy-start.7
  1.5 0.9 copy-done.7
  2.4 2.8 %shard_map.102 = bf16[2048,128]{1,0:T(8,128)(2,1)} custom-call(s32[128,32]{1,0:T(8,128)S(1)} %copy.11.index_ref, bf16[128,1024]{1,0:T(8,128)(2,1)S(1)} %copy-done.7), custom_call_target="tpu_custom_call" | custom-call | flops 536870912 | bytes 802816 | tf_op jit(solution)/shard_map/pallas_call | solution.py:30
  5.2 17.8 %all-to-all-start = ((bf16[32,64,128]{2,1,0:T(8,128)(2,1)}), bf16[32,64,128]{2,1,0:T(8,128)(2,1)S(1)}, u32[]{:S(2)}, u32[]{:S(2)}) async-start(bf16[32,64,128]{2,1,0:T(8,128)(2,1)} %bitcast), calls=%async_computation | async-start | bytes 1048576 | tf_op jit(solution)/shard_map/all_to_all | solution.py:238
  23.1 1.6 %shard_map.101 = (bf16[32,32,128]{2,1,0:T(8,128)(2,1)S(1)}, f32[64,128]{1,0:T(8,128)S(1)}, s32[32,128]{1,0:T(8,128)S(1)}) custom-call(s32[128,32]{1,0:T(8,128)S(1)} %copy.11.index_ref, bf16[128,1024]{1,0:T(8,128)(2,1)S(1)} %copy-done.8), custom_call_target="tpu_custom_call" | custom-call | flops 268435456 | bytes 589824 | tf_op jit(solution)/shard_map/pallas_call | solution.py:30
  24.7 9.5 %all-to-all-done.got_ref = bf16[32,64,128]{2,1,0:T(8,128)(2,1)S(1)} async-done(((bf16[32,64,128]{2,1,0:T(8,128)(2,1)}), bf16[32,64,128]{2,1,0:T(8,128)(2,1)S(1)}, u32[]{:S(2)}, u32[]{:S(2)}) %all-to-all-start) | async-done | bytes 524320 | tf_op jit(solution)/shard_map/all_to_all | solution.py:238
  34.2 0.1 shard_map.103
  34.3 30.5 %all_to_all.30.got_ref = bf16[32,50,128]{2,1,0:T(8,128)(2,1)S(1)} all-to-all(bf16[32,50,128]{2,1,0:T(8,128)(2,1)S(1)} %shard_map.103), channel_id=1, replica_groups={{0,1,2,3,4,5,6,7,8,9,10,11,12,13,14,15,16,17,18,19,20,21,22,23,24,25,26..., dimensions={0} | all-to-all | bytes 819200 | tf_op jit(solution)/shard_map/all_to_all | solution.py:277
  64.8 0.9 shard_map.104
  65.7 0.0 copy-start.2
  65.7 9.3 %all_to_all.31.got_ref = bf16[8,128,128]{2,1,0:T(8,128)(2,1)S(1)} all-to-all(bf16[8,128,128]{2,1,0:T(8,128)(2,1)S(1)} %bitcast.4), channel_id=1, replica_groups=mesh['x'=4,'z_hi'=4,'core'=2,'z_lo'=8,'y'=4] {'x','core'}, dimensions={0} | all-to-all | bytes 524288 | tf_op jit(solution)/shard_map/all_to_all | solution.py:238
  75.1 10.8 %collective-permute-start = (bf16[192,128]{1,0:T(8,128)(2,1)S(1)}, bf16[192,128]{1,0:T(8,128)(2,1)S(1)}, u32[]{:S(2)}, u32[]{:S(2)}) collective-permute-start(bf16[192,128]{1,0:T(8,128)(2,1)S(1)} %shard_map.105.a_ref.after_ref), channel_id=1, source_target_pairs={{0,64},{4,68},{8,72},{12,76},{16,80},{20,84},{24,88},{28,92},{64,0... | collective-permute-start | bytes 147464 | tf_op jit(solution)/shard_map/ppermute | solution.py:273
  85.9 1.5 %shard_map.107 = bf16[32,32,128]{2,1,0:T(8,128)(2,1)} custom-call(s32[8,128]{1,0:T(8,128)S(1)} %get-tuple-element.24.wanted_ref, f32[1024,128]{1,0:T(8,128)S(1)} %copy-done.2, bf16[192,128]{1,0:T(8,128)(2,1)S(1)} %shard_map.105.a_ref.after_ref), custom_call_target="tpu_custom_call" | custom-call | flops 268435456 | bytes 839680 | tf_op jit(solution)/shard_map/pallas_call | solution.py:30
  87.4 4.6 %all-to-all-start.3 = ((bf16[32,32,128]{2,1,0:T(8,128)(2,1)}), bf16[32,32,128]{2,1,0:T(8,128)(2,1)}, u32[]{:S(2)}, u32[]{:S(2)}) async-start(bf16[32,32,128]{2,1,0:T(8,128)(2,1)} %shard_map.107), calls=%async_computation.3 | async-start | bytes 524288 | tf_op jit(solution)/shard_map/all_to_all | solution.py:277
  92.0 0.0 collective-permute-done.b_ref
  92.0 0.0 copy-start
  92.0 0.0 copy-start.6
  92.1 8.1 %collective-permute-start.1 = (bf16[192,128]{1,0:T(8,128)(2,1)S(1)}, bf16[192,128]{1,0:T(8,128)(2,1)S(1)}, u32[]{:S(2)}, u32[]{:S(2)}) collective-permute-start(bf16[192,128]{1,0:T(8,128)(2,1)S(1)} %shard_map.106.mine_ref), channel_id=1, source_target_pairs={{0,192},{4,196},{8,200},{12,204},{16,208},{20,212},{24,216},{28,22... | collective-permute-start | bytes 147464 | tf_op jit(solution)/shard_map/ppermute | solution.py:273
  100.2 2.0 %shard_map.108.part_ref.after_ref = f32[1024,128]{1,0:T(8,128)S(1)} custom-call(s32[128,32]{1,0:T(8,128)S(1)} %copy-done.6, f32[2048,128]{1,0:T(8,128)S(1)} %copy-done), custom_call_target="tpu_custom_call" | custom-call | flops 536870912 | bytes 1589248 | tf_op jit(solution)/shard_map/pallas_call | solution.py:30
  102.2 5.3 %collective-permute-done.1.got_ref = bf16[192,128]{1,0:T(8,128)(2,1)S(1)} collective-permute-done((bf16[192,128]{1,0:T(8,128)(2,1)S(1)}, bf16[192,128]{1,0:T(8,128)(2,1)S(1)}, u32[]{:S(2)}, u32[]{:S(2)}) %collective-permute-start.1) | collective-permute-done | bytes 49184 | tf_op jit(solution)/shard_map/ppermute | solution.py:273
  107.5 0.0 all-to-all-done.3
  107.5 8.0 %all_to_all.32.got_ref = bf16[4,64,128]{2,1,0:T(8,128)(2,1)S(1)} all-to-all(bf16[4,64,128]{2,1,0:T(8,128)(2,1)S(1)} %get-tuple-element.27), channel_id=1, replica_groups=mesh['x'=4,'z_hi'=4,'core'=2,'z_lo'=8,'y'=4] {'y'}, dimensions={0} | all-to-all | bytes 131072 | tf_op jit(solution)/shard_map/all_to_all | solution.py:238
  115.6 0.1 shard_map.111
  115.6 8.6 %all_to_all.33.mine_ref = bf16[4,384,128]{2,1,0:T(8,128)(2,1)S(1)} all-to-all(bf16[4,384,128]{2,1,0:T(8,128)(2,1)S(1)} %shard_map.111), channel_id=1, replica_groups=mesh['x'=4,'z_hi'=4,'core'=2,'z_lo'=8,'y'=4] {'x'}, dimensions={0} | all-to-all | bytes 786432 | tf_op jit(solution)/shard_map/all_to_all | solution.py:238
  124.2 8.1 %collective-permute-start.2 = (bf16[4,384,128]{2,1,0:T(8,128)(2,1)S(1)}, bf16[4,384,128]{2,1,0:T(8,128)(2,1)S(1)}, u32[]{:S(2)}, u32[]{:S(2)}) collective-permute-start(bf16[4,384,128]{2,1,0:T(8,128)(2,1)S(1)} %all_to_all.33.mine_ref), channel_id=1, source_target_pairs={{0,32},{32,0},{1,33},{33,1},{2,34},{34,2},{3,35},{35,3},{4,36},{36... | collective-permute-start | bytes 1179656 | tf_op jit(solution)/shard_map/ppermute | solution.py:337
  132.4 0.0 copy-start.3
  132.4 0.0 copy-start.4
  132.4 2.7 %shard_map.109 = bf16[128,1024]{1,0:T(8,128)(2,1)} custom-call(s32[32,128]{1,0:T(8,128)S(1)} %get-tuple-element.19.slot_ref, bf16[1024,128]{1,0:T(8,128)(2,1)} %bitcast.2.rows_ref, f32[1024,128]{1,0:T(8,128)S(1)} %shard_map.108.part_ref.after_ref), custom_call_target="tpu_custom_call" | custom-call | flops 268435456 | bytes 1064960 | tf_op jit(solution)/shard_map/pallas_call | solution.py:30
  135.1 0.0 collective-permute-done.2.other_ref
  135.2 1.2 shard_map.113
  136.4 1.8 %shard_map.112 = (f32[2048,128]{1,0:T(8,128)}, f32[2048,128]{1,0:T(8,128)}) custom-call(s32[1]{0:T(128)} %bitcast.3.core_ref, bf16[4,384,128]{2,1,0:T(8,128)(2,1)S(1)} %all_to_all.33.mine_ref, bf16[4,384,128]{2,1,0:T(8,128)(2,1)S(1)} %collective-permute-done.2.other_ref, f32[2048,128]{1,0:T(8,128)S(1)} %copy-done, f32[2048,128]{1,0:T(8,128)S(1)} %copy-done.1), custom_call_target="tpu_custom_call" | custom-call | bytes 4980740 | tf_op jit(solution)/shard_map/pallas_call | solution.py:30
  (14 shorter events, 0.1 us)
Async XLA Ops:
  1.4 1.0 copy-start.7
  2.4 20.7 %copy-start.5 = (s32[128,32]{1,0:T(8,128)}, s32[128,32]{1,0:T(8,128)S(1)}, u32[]{:S(2)}) copy-start(s32[128,32]{1,0:T(8,128)S(1)} %copy.11.index_ref) | copy-start | bytes 49156
  5.2 17.9 %copy-start.8 = (bf16[128,1024]{1,0:T(8,128)(2,1)S(1)}, bf16[128,1024]{1,0:T(8,128)(2,1)}, u32[]{:S(2)}) copy-start(bf16[128,1024]{1,0:T(8,128)(2,1)} %grad_ref.3) | copy-start | bytes 786436
  5.2 29.0 %all-to-all-start = ((bf16[32,64,128]{2,1,0:T(8,128)(2,1)}), bf16[32,64,128]{2,1,0:T(8,128)(2,1)S(1)}, u32[]{:S(2)}, u32[]{:S(2)}) async-start(bf16[32,64,128]{2,1,0:T(8,128)(2,1)} %bitcast), calls=%async_computation | async-start | bytes 1048576 | tf_op jit(solution)/shard_map/all_to_all | solution.py:238
  65.7 20.2 %copy-start.2 = (f32[1024,128]{1,0:T(8,128)S(1)}, f32[1024,128]{1,0:T(8,128)}, u32[]{:S(2)}) copy-start(f32[1024,128]{1,0:T(8,128)} %rows_ref.7) | copy-start | bytes 1572868
  75.1 16.9 %collective-permute-start = (bf16[192,128]{1,0:T(8,128)(2,1)S(1)}, bf16[192,128]{1,0:T(8,128)(2,1)S(1)}, u32[]{:S(2)}, u32[]{:S(2)}) collective-permute-start(bf16[192,128]{1,0:T(8,128)(2,1)S(1)} %shard_map.105.a_ref.after_ref), channel_id=1, source_target_pairs={{0,64},{4,68},{8,72},{12,76},{16,80},{20,84},{24,88},{28,92},{64,0... | collective-permute-start | bytes 147464 | tf_op jit(solution)/shard_map/ppermute | solution.py:273
  87.4 20.1 %all-to-all-start.3 = ((bf16[32,32,128]{2,1,0:T(8,128)(2,1)}), bf16[32,32,128]{2,1,0:T(8,128)(2,1)}, u32[]{:S(2)}, u32[]{:S(2)}) async-start(bf16[32,32,128]{2,1,0:T(8,128)(2,1)} %shard_map.107), calls=%async_computation.3 | async-start | bytes 524288 | tf_op jit(solution)/shard_map/all_to_all | solution.py:277
  92.0 8.2 %copy-start = (f32[2048,128]{1,0:T(8,128)S(1)}, f32[2048,128]{1,0:T(8,128)}, u32[]{:S(2)}) copy-start(f32[2048,128]{1,0:T(8,128)} %rows_ref.6) | copy-start | bytes 3145732
  92.0 8.2 %copy-start.6 = (s32[128,32]{1,0:T(8,128)S(1)}, s32[128,32]{1,0:T(8,128)}, u32[]{:S(2)}) copy-start(s32[128,32]{1,0:T(8,128)} %copy-done.5) | copy-start | bytes 49156
  92.1 15.4 %collective-permute-start.1 = (bf16[192,128]{1,0:T(8,128)(2,1)S(1)}, bf16[192,128]{1,0:T(8,128)(2,1)S(1)}, u32[]{:S(2)}, u32[]{:S(2)}) collective-permute-start(bf16[192,128]{1,0:T(8,128)(2,1)S(1)} %shard_map.106.mine_ref), channel_id=1, source_target_pairs={{0,192},{4,196},{8,200},{12,204},{16,208},{20,212},{24,216},{28,22... | collective-permute-start | bytes 147464 | tf_op jit(solution)/shard_map/ppermute | solution.py:273
  124.2 10.9 %collective-permute-start.2 = (bf16[4,384,128]{2,1,0:T(8,128)(2,1)S(1)}, bf16[4,384,128]{2,1,0:T(8,128)(2,1)S(1)}, u32[]{:S(2)}, u32[]{:S(2)}) collective-permute-start(bf16[4,384,128]{2,1,0:T(8,128)(2,1)S(1)} %all_to_all.33.mine_ref), channel_id=1, source_target_pairs={{0,32},{32,0},{1,33},{33,1},{2,34},{34,2},{3,35},{35,3},{4,36},{36... | collective-permute-start | bytes 1179656 | tf_op jit(solution)/shard_map/ppermute | solution.py:337
  132.4 2.8 %copy-start.3 = (f32[1024,128]{1,0:T(8,128)S(1)}, f32[1024,128]{1,0:T(8,128)}, u32[]{:S(2)}) copy-start(f32[1024,128]{1,0:T(8,128)} %rows_ref.7) | copy-start | bytes 1572868
  132.4 2.8 %copy-start.4 = (f32[1024,128]{1,0:T(8,128)S(1)}, f32[1024,128]{1,0:T(8,128)}, u32[]{:S(2)}) copy-start(f32[1024,128]{1,0:T(8,128)} %history_ref.3) | copy-start | bytes 1572868
  135.1 1.3 copy-start.1

commit v5 on v4

--- a/solution.py
+++ b/solution.py
@@ -15,8 +15,8 @@
 CAP = 32
 OWNERS = 32
 BLOCK = 256
-QUARTER = NF // 128
-MSG = CAP + QUARTER + 2
+PIECE = NF // 256
+MSG = CAP + PIECE + 2
 PAIR_COST = 10**12
 BF = jnp.bfloat16
 F32 = jnp.float32
@@ -62,16 +62,39 @@
     return jnp.concatenate([grad[:, f * E : (f + 1) * E] for f in range(F)], axis=0)
 
 
-def frequent_kernel(index_ref, grad_ref, part_ref):
-    index = index_ref[...].T
+def frequent_kernel(index_hbm, grad_hbm, part_ref, index_ref, grad_ref, sems):
+    index_copy = pltpu.make_async_copy(index_hbm, index_ref, sems.at[0])
+    grad_copy = pltpu.make_async_copy(grad_hbm, grad_ref, sems.at[1])
+    index_copy.start()
+    grad_copy.start()
+    index_copy.wait()
+    index = index_ref[...]
+    first = counts(index, 0)
+    grad_copy.wait()
     grad = stack_tables(grad_ref[...])
     for base in range(0, NF, BLOCK):
-        part = jnp.dot(counts(index, base), grad, preferred_element_type=F32)
+        hits = counts(index, base) if base else first
+        part = jnp.dot(hits, grad, preferred_element_type=F32)
         part_ref[base : base + BLOCK, :] = part.astype(BF)
 
 
+def frequent_part(index, grad):
+    return pl.pallas_call(
+        frequent_kernel,
+        out_shape=sds((NF, E), BF),
+        in_specs=[pl.BlockSpec(memory_space=pl.ANY)] * 2,
+        out_specs=pl.BlockSpec(memory_space=pltpu.VMEM),
+        scratch_shapes=[
+            pltpu.VMEM(index.shape, index.dtype),
+            pltpu.VMEM(grad.shape, grad.dtype),
+            pltpu.SemaphoreType.DMA((2,)),
+        ],
+        compiler_params=pltpu.CompilerParams(vmem_limit_bytes=60 * 1024 * 1024),
+    )(index, grad)
+
+
 def slots_kernel(index_ref, grad_ref, out_ref, req_ref, slot_ref):
-    index = index_ref[...].T
+    index = index_ref[...]
     remote = index >= NF
     offset = index - NF
     owner = jnp.where(remote, offset // RO, -1)
@@ -117,10 +140,10 @@
 def message_kernel(slots_ref, req_ref, got_ref, msg_ref):
     part = jnp.sum(got_ref[...].astype(F32), axis=0)
     for t in range(OWNERS):
-        row = t % 4 * QUARTER
+        row = (t % 4 * 2 + t // 4 % 2) * PIECE
         high = req_ref[t : t + 1, :]
         low = req_ref[OWNERS + t : OWNERS + t + 1, :]
-        tail = jnp.concatenate([part[row : row + QUARTER], high, low], axis=0).astype(BF)
+        tail = jnp.concatenate([part[row : row + PIECE], high, low], axis=0).astype(BF)
         msg_ref[t] = jnp.concatenate([slots_ref[t], tail], axis=0)
 
 
@@ -130,10 +153,10 @@
 
 def owner_kernel(got_ref, part_ref, wanted_ref, freq_ref):
     tails = [got_ref[t].astype(F32)[CAP:] for t in range(OWNERS)]
-    quarters = [sum(t[:QUARTER] for t in tails[y::4]) for y in range(4)]
-    freq_ref[...] = jnp.concatenate(quarters, axis=0).astype(BF)
-    high = jnp.concatenate([t[QUARTER : QUARTER + 1] for t in tails], axis=0)
-    low = jnp.concatenate([t[QUARTER + 1 :] for t in tails], axis=0)
+    pieces = [sum(t[:PIECE] for t in tails[y::4]) for y in range(4)]
+    freq_ref[...] = jnp.concatenate(pieces, axis=0).astype(BF)
+    high = jnp.concatenate([t[PIECE : PIECE + 1] for t in tails], axis=0)
+    low = jnp.concatenate([t[PIECE + 1 :] for t in tails], axis=0)
     source = lax.broadcasted_iota(jnp.int32, (OWNERS, E), 0) % 4
 
     def placed(x):
@@ -180,21 +203,25 @@
     del after_ref
     total = (mine_ref[...].astype(F32) + got_ref[...].astype(F32)).astype(BF)
     owned_ref[...] = total[: RO // 8]
-    for i in range(4):
+    for i in range(8):
         freq_ref[i] = total[RO // 8 :]
 
 
 def spread_kernel(got_ref, owned_ref, out_ref):
+    got = [got_ref[k].astype(F32) for k in range(8)]
     freq = [
-        got_ref[q, y * QUARTER : (y + 1) * QUARTER, :] for y in range(4) for q in range(4)
+        got[p * 4 + q][y * PIECE : (y + 1) * PIECE]
+        for y in range(4)
+        for q in range(4)
+        for p in range(2)
     ]
-    rows = jnp.concatenate(freq + [owned_ref[...]], axis=0)
+    rows = jnp.concatenate([jnp.concatenate(freq, axis=0).astype(BF), owned_ref[...]], axis=0)
     for i in range(4):
         out_ref[i] = rows
 
 
 def pool_frequent_kernel(index_ref, rows_ref, out_ref):
-    index = index_ref[...].T
+    index = index_ref[...]
     total = jnp.zeros((F * B, E), F32)
     for base in range(0, NF, BLOCK):
         rows = rows_ref[base : base + BLOCK, :].astype(BF)
@@ -262,7 +289,7 @@
     pairs = []
     for core in range(2):
         for w in range(4):
-            other = w ^ 1 if core == step else (3 - w) % 4
+            other = w ^ 1 if step == 0 else (3 - w) % 4
             for z in range(8):
                 a, b = z_hi_of(w, core, z), z_hi_of(other, core, z)
                 pairs.append(((a * 2 + core) * 8 + z, (b * 2 + core) * 8 + z))
@@ -270,13 +297,13 @@
 
 
 def far(x, step):
-    return lax.ppermute(x, ("z_hi", "core", "z_lo"), far_pairs(step))
+    return lax.ppermute(x, ("z_hi", "core", "z_pair", "z_odd"), far_pairs(step))
 
 
 def to_owners(x):
     return lax.all_to_all(
         x,
-        ("z_hi", "core", "z_lo", "y"),
+        ("z_hi", "core", "z_pair", "z_odd", "y"),
         split_axis=0,
         concat_axis=0,
         tiled=True,
@@ -285,11 +312,10 @@
 
 
 def body(index, frequent_rows, frequent_history, owned_rows, owned_history, grad):
+    index = index.T
     near, plane = ("x", "core"), ("x", "core", "y")
     flat = F * B
-    part = call(
-        frequent_kernel, [sds((NF, E), BF)], index, grad, flops=2 * NF * flat * E
-    )[0]
+    part = frequent_part(index, grad)
     part = swap(part.reshape(32, NF // 32, E), plane)
     slots, req, slot = call(
         slots_kernel,
@@ -306,12 +332,12 @@
     got = to_owners(msg)
     owned, wanted, freq = call(
         owner_kernel,
-        [sds((RO, E), BF), sds((8, E), jnp.int32), sds((NF // 32, E), BF)],
+        [sds((RO, E), BF), sds((8, E), jnp.int32), sds((NF // 64, E), BF)],
         got,
         flops=2 * RO * RO * E,
     )
     owned = swap(owned.reshape(8, RO // 8, E), near)
-    both = call(slice_kernel, [sds((RO // 8 + NF // 32, E), BF)], owned, freq)[0]
+    both = call(slice_kernel, [sds((RO // 8 + NF // 64, E), BF)], owned, freq)[0]
     served = call(
         serve_kernel,
         [sds((OWNERS, CAP, E), BF)],
@@ -329,9 +355,9 @@
         pool_frequent_kernel, [sds((flat, E), F32)], index, frequent_rows, flops=2 * NF * flat * E
     )[0]
     owned, freq = call(
-        total_kernel, [sds((RO // 8, E), BF), sds((4, NF // 32, E), BF)], both, got, pooled
-    )
-    freq = swap(freq, "y")
+        total_kernel, [sds((RO // 8, E), BF), sds((8, NF // 64, E), BF)], both, got, pooled
+    )
+    freq = swap(freq, ("z_odd", "y"))
     both = call(spread_kernel, [sds((4, (NF + RO) // 8, E), BF)], freq, owned)[0]
     mine = swap(both, "x")
     other = lax.ppermute(mine, "core", [(0, 1), (1, 0)])
@@ -354,8 +380,9 @@
 
 
 def solution(mesh):
-    fine = Mesh(mesh.devices.reshape(4, 4, 2, 8, 4), ("x", "z_hi", "core", "z_lo", "y"))
-    samples, table = ("x", "z_hi", "core", "z_lo", "y"), ("z_lo", "y")
+    names = ("x", "z_hi", "core", "z_pair", "z_odd", "y")
+    fine = Mesh(mesh.devices.reshape(4, 4, 2, 4, 2, 4), names)
+    samples, table = names, names[3:]
     in_specs = (P(samples, None), P(), P(), P(table, None), P(table, None), P(samples, None))
     out_specs = (P(samples, None), P(), P(table, None), P(), P(table, None))
     return jax.shard_map(body, mesh=fine, in_specs=in_specs, out_specs=out_specs, check_vma=False)

time: 140 us -> 137 us (0.979)
  waiting for transfers between devices: 14.8 us -> 12.1 us
  local copies, waits for them, and re-layouts: 1.8 us -> 0.04 us
    pallas_call x0 -> x1, Pallas kernels: none -> 3.64 us  [frequent_part(): pl.pallas_call(frequent_kernel, out_shape=sds((NF, E), BF), in_specs=[pl....]
    ppermute x2, waiting for transfers between devices: 5.3 us -> 2.46 us  [far(): return lax.ppermute(x, ('z_hi', 'core', 'z_pair', 'z_odd'), far_pairs(step))]
    all_to_all x3, blocking collectives: 26 us -> 28.6 us  [swap(): return lax.all_to_all(x, axes, split_axis=0, concat_axis=0, tiled=True)]
    pallas_call x13 -> x12, Pallas kernels: 14.8 us -> 12.3 us  [call(): pl.pallas_call(kernel, out_shape=outs, in_specs=[pl.BlockSpec(memory_spac...]
    all_to_all x1, blocking collectives: 30.5 us -> 28.1 us  [to_owners(): lax.all_to_all(x, ('z_hi', 'core', 'z_pair', 'z_odd', 'y'), split_axis=0,...]
    ppermute x2, starting transfers between devices: 18.9 us -> 20.7 us  [far(): return lax.ppermute(x, ('z_hi', 'core', 'z_pair', 'z_odd'), far_pairs(step))]
    unnamed x19 -> x14, local copies, waits for them, and re-layouts: 1.8 us -> 0.04 us
where the time goes in v5:
time: 137 us; the launch traced here: 136 us
  blocking collectives  56.7 us (41%)
  starting transfers between devices  50.6 us (37%)
  Pallas kernels  15.9 us (12%)
  waiting for transfers between devices  12.1 us (9%)
    all_to_all x3, blocking collectives, swap(): return lax.all_to_all(x, axes, split_axis=0, concat_axis=0, tiled=True)  28.6 us
    all_to_all x1, blocking collectives, to_owners(): lax.all_to_all(x, ('z_hi', 'core', 'z_pair', 'z_odd', 'y'), split_axis=0,...  28.1 us
    ppermute x2, starting transfers between devices, far(): return lax.ppermute(x, ('z_hi', 'core', 'z_pair', 'z_odd'), far_pairs(step))  20.7 us
    all_to_all x1, starting transfers between devices, swap(): return lax.all_to_all(x, axes, split_axis=0, concat_axis=0, tiled=True)  17.9 us
    pallas_call x12, Pallas kernels, call(): pl.pallas_call(kernel, out_shape=outs, in_specs=[pl.BlockSpec(memory_spac...  12.3 us
    all_to_all x1, waiting for transfers between devices, swap(): return lax.all_to_all(x, axes, split_axis=0, concat_axis=0, tiled=True)  9.58 us
    ppermute x1, starting transfers between devices, body(): other = lax.ppermute(mine, 'core', [(0, 1), (1, 0)])  7.38 us
    all_to_all x1, starting transfers between devices, to_owners(): lax.all_to_all(x, ('z_hi', 'core', 'z_pair', 'z_odd', 'y'), split_axis=0,...  4.69 us
  transfers between devices with their start and end apart: 5, of which 2 were waited for; matrix products, arithmetic and copies ran while one was open for 0% of the time, Pallas kernels for 6%

profile of v5, /device:TPU:1, one launch (start us, length us, event | category | flops | bytes accessed | tf_op | source)
XLA Modules:
  0.0 136.2 jit_solution(11453505341685879751)
XLA Ops:
  0.6 3.6 %shard_map.102 = bf16[2048,128]{1,0:T(8,128)(2,1)} custom-call(s32[32,128]{1,0:T(8,128)} %bitcast.6, bf16[128,1024]{1,0:T(8,128)(2,1)} %grad_hbm.1), custom_call_target="tpu_custom_call" | custom-call | tf_op jit(solution)/shard_map/pallas_call | solution.py:82
  4.3 0.0 copy-start.5
  4.3 0.0 copy-start.6
  4.3 17.9 %all-to-all-start = ((bf16[32,64,128]{2,1,0:T(8,128)(2,1)}), bf16[32,64,128]{2,1,0:T(8,128)(2,1)S(1)}, u32[]{:S(2)}, u32[]{:S(2)}) async-start(bf16[32,64,128]{2,1,0:T(8,128)(2,1)} %bitcast.9), calls=%async_computation | async-start | bytes 1048576 | tf_op jit(solution)/shard_map/all_to_all | solution.py:265
  22.2 1.5 %shard_map.101 = (bf16[32,32,128]{2,1,0:T(8,128)(2,1)S(1)}, f32[64,128]{1,0:T(8,128)S(1)}, s32[32,128]{1,0:T(8,128)S(1)}) custom-call(s32[32,128]{1,0:T(8,128)S(1)} %bitcast.7, bf16[128,1024]{1,0:T(8,128)(2,1)S(1)} %copy-done.5), custom_call_target="tpu_custom_call" | custom-call | flops 268435456 | bytes 589824 | tf_op jit(solution)/shard_map/pallas_call | solution.py:30
  23.7 9.6 %all-to-all-done.got_ref = bf16[32,64,128]{2,1,0:T(8,128)(2,1)S(1)} async-done(((bf16[32,64,128]{2,1,0:T(8,128)(2,1)}), bf16[32,64,128]{2,1,0:T(8,128)(2,1)S(1)}, u32[]{:S(2)}, u32[]{:S(2)}) %all-to-all-start) | async-done | bytes 524320 | tf_op jit(solution)/shard_map/all_to_all | solution.py:265
  33.3 0.1 shard_map.103
  33.4 28.1 %all_to_all.30.got_ref = bf16[32,42,128]{2,1,0:T(8,128)(2,1)S(1)} all-to-all(bf16[32,42,128]{2,1,0:T(8,128)(2,1)S(1)} %shard_map.103), channel_id=1, replica_groups={{0,1,2,3,4,5,6,7,8,9,10,11,12,13,14,15,16,17,18,19,20,21,22,23,24,25,26..., dimensions={0} | all-to-all | bytes 688128 | tf_op jit(solution)/shard_map/all_to_all | solution.py:304
  61.5 0.9 shard_map.104
  62.4 0.0 copy-start.2
  62.5 9.1 %all_to_all.31.got_ref = bf16[8,128,128]{2,1,0:T(8,128)(2,1)S(1)} all-to-all(bf16[8,128,128]{2,1,0:T(8,128)(2,1)S(1)} %bitcast.5), channel_id=1, replica_groups=mesh['x'=4,'z_hi'=4,'core'=2,'z_pair'=4,'z_odd'=2,'y'=4] {'x','core'}, dimensions={0} | all-to-all | bytes 524288 | tf_op jit(solution)/shard_map/all_to_all | solution.py:265
  71.6 11.3 %collective-permute-start = (bf16[160,128]{1,0:T(8,128)(2,1)S(1)}, bf16[160,128]{1,0:T(8,128)(2,1)S(1)}, u32[]{:S(2)}, u32[]{:S(2)}) collective-permute-start(bf16[160,128]{1,0:T(8,128)(2,1)S(1)} %shard_map.105.a_ref.after_ref), channel_id=1, source_target_pairs={{0,64},{4,68},{8,72},{12,76},{16,80},{20,84},{24,88},{28,92},{64,0... | collective-permute-start | bytes 122888 | tf_op jit(solution)/shard_map/ppermute | solution.py:300
  82.9 0.0 copy-done.2
  82.9 1.5 %shard_map.107 = bf16[32,32,128]{2,1,0:T(8,128)(2,1)} custom-call(s32[8,128]{1,0:T(8,128)S(1)} %get-tuple-element.24.wanted_ref, f32[1024,128]{1,0:T(8,128)S(1)} %copy-done.2, bf16[160,128]{1,0:T(8,128)(2,1)S(1)} %shard_map.105.a_ref.after_ref), custom_call_target="tpu_custom_call" | custom-call | flops 268435456 | bytes 831488 | tf_op jit(solution)/shard_map/pallas_call | solution.py:30
  84.3 4.7 %all-to-all-start.3 = ((bf16[32,32,128]{2,1,0:T(8,128)(2,1)}), bf16[32,32,128]{2,1,0:T(8,128)(2,1)}, u32[]{:S(2)}, u32[]{:S(2)}) async-start(bf16[32,32,128]{2,1,0:T(8,128)(2,1)} %shard_map.107), calls=%async_computation.3 | async-start | bytes 524288 | tf_op jit(solution)/shard_map/all_to_all | solution.py:304
  89.0 0.0 collective-permute-done.b_ref
  89.1 0.0 copy-start
  89.1 9.5 %collective-permute-start.1 = (bf16[160,128]{1,0:T(8,128)(2,1)S(1)}, bf16[160,128]{1,0:T(8,128)(2,1)S(1)}, u32[]{:S(2)}, u32[]{:S(2)}) collective-permute-start(bf16[160,128]{1,0:T(8,128)(2,1)S(1)} %shard_map.106.mine_ref), channel_id=1, source_target_pairs={{0,192},{4,196},{8,200},{12,204},{16,208},{20,212},{24,216},{28,22... | collective-permute-start | bytes 122888 | tf_op jit(solution)/shard_map/ppermute | solution.py:300
  98.5 0.0 copy-done
  98.6 2.3 %shard_map.108.part_ref.after_ref = f32[1024,128]{1,0:T(8,128)S(1)} custom-call(s32[32,128]{1,0:T(8,128)S(1)} %bitcast.8, f32[2048,128]{1,0:T(8,128)S(1)} %copy-done), custom_call_target="tpu_custom_call" | custom-call | flops 536870912 | bytes 1589248 | tf_op jit(solution)/shard_map/pallas_call | solution.py:30
  100.9 2.5 %collective-permute-done.1.got_ref = bf16[160,128]{1,0:T(8,128)(2,1)S(1)} collective-permute-done((bf16[160,128]{1,0:T(8,128)(2,1)S(1)}, bf16[160,128]{1,0:T(8,128)(2,1)S(1)}, u32[]{:S(2)}, u32[]{:S(2)}) %collective-permute-start.1) | collective-permute-done | bytes 40992 | tf_op jit(solution)/shard_map/ppermute | solution.py:300
  103.4 0.0 all-to-all-done.3
  103.4 10.9 %all_to_all.32.got_ref = bf16[8,32,128]{2,1,0:T(8,128)(2,1)S(1)} all-to-all(bf16[8,32,128]{2,1,0:T(8,128)(2,1)S(1)} %get-tuple-element.27), channel_id=1, replica_groups=mesh['x'=4,'z_hi'=4,'core'=2,'z_pair'=4,'z_odd'=2,'y'=4] {'z_odd','y'}, dimensions={0} | all-to-all | bytes 131072 | tf_op jit(solution)/shard_map/all_to_all | solution.py:265
  114.3 0.1 shard_map.111
  114.4 8.6 %all_to_all.33.mine_ref = bf16[4,384,128]{2,1,0:T(8,128)(2,1)S(1)} all-to-all(bf16[4,384,128]{2,1,0:T(8,128)(2,1)S(1)} %shard_map.111), channel_id=1, replica_groups=mesh['x'=4,'z_hi'=4,'core'=2,'z_pair'=4,'z_odd'=2,'y'=4] {'x'}, dimensions={0} | all-to-all | bytes 786432 | tf_op jit(solution)/shard_map/all_to_all | solution.py:265
  123.0 7.4 %collective-permute-start.2 = (bf16[4,384,128]{2,1,0:T(8,128)(2,1)S(1)}, bf16[4,384,128]{2,1,0:T(8,128)(2,1)S(1)}, u32[]{:S(2)}, u32[]{:S(2)}) collective-permute-start(bf16[4,384,128]{2,1,0:T(8,128)(2,1)S(1)} %all_to_all.33.mine_ref), channel_id=1, source_target_pairs={{0,32},{32,0},{1,33},{33,1},{2,34},{34,2},{3,35},{35,3},{4,36},{36... | collective-permute-start | bytes 1179656 | tf_op jit(solution)/shard_map/ppermute | solution.py:363
  130.4 0.0 copy-start.3
  130.4 0.0 copy-start.4
  130.4 2.7 %shard_map.109 = bf16[128,1024]{1,0:T(8,128)(2,1)} custom-call(s32[32,128]{1,0:T(8,128)S(1)} %get-tuple-element.19.slot_ref, bf16[1024,128]{1,0:T(8,128)(2,1)} %bitcast.3.rows_ref, f32[1024,128]{1,0:T(8,128)S(1)} %shard_map.108.part_ref.after_ref), custom_call_target="tpu_custom_call" | custom-call | flops 268435456 | bytes 1064960 | tf_op jit(solution)/shard_map/pallas_call | solution.py:30
  133.1 0.0 collective-permute-done.2.other_ref
  133.2 1.2 shard_map.113
  134.4 1.8 %shard_map.112 = (f32[2048,128]{1,0:T(8,128)}, f32[2048,128]{1,0:T(8,128)}) custom-call(s32[1]{0:T(128)} %bitcast.4.core_ref, bf16[4,384,128]{2,1,0:T(8,128)(2,1)S(1)} %all_to_all.33.mine_ref, bf16[4,384,128]{2,1,0:T(8,128)(2,1)S(1)} %collective-permute-done.2.other_ref, f32[2048,128]{1,0:T(8,128)S(1)} %copy-done, f32[2048,128]{1,0:T(8,128)S(1)} %copy-done.1), custom_call_target="tpu_custom_call" | custom-call | bytes 4980740 | tf_op jit(solution)/shard_map/pallas_call | solution.py:30
  (9 shorter events, 0.1 us)
Async XLA Ops:
  4.3 17.9 %copy-start.5 = (bf16[128,1024]{1,0:T(8,128)(2,1)S(1)}, bf16[128,1024]{1,0:T(8,128)(2,1)}, u32[]{:S(2)}) copy-start(bf16[128,1024]{1,0:T(8,128)(2,1)} %grad_hbm.1) | copy-start | bytes 786436
  4.3 17.9 %copy-start.6 = (s32[128,32]{0,1:T(8,128)S(1)}, s32[128,32]{0,1:T(8,128)}, u32[]{:S(2)}) copy-start(s32[128,32]{0,1:T(8,128)} %param.6) | copy-start | bytes 49156
  4.3 29.0 %all-to-all-start = ((bf16[32,64,128]{2,1,0:T(8,128)(2,1)}), bf16[32,64,128]{2,1,0:T(8,128)(2,1)S(1)}, u32[]{:S(2)}, u32[]{:S(2)}) async-start(bf16[32,64,128]{2,1,0:T(8,128)(2,1)} %bitcast.9), calls=%async_computation | async-start | bytes 1048576 | tf_op jit(solution)/shard_map/all_to_all | solution.py:265
  62.4 20.4 %copy-start.2 = (f32[1024,128]{1,0:T(8,128)S(1)}, f32[1024,128]{1,0:T(8,128)}, u32[]{:S(2)}) copy-start(f32[1024,128]{1,0:T(8,128)} %rows_ref.7) | copy-start | bytes 1572868
  71.6 17.5 %collective-permute-start = (bf16[160,128]{1,0:T(8,128)(2,1)S(1)}, bf16[160,128]{1,0:T(8,128)(2,1)S(1)}, u32[]{:S(2)}, u32[]{:S(2)}) collective-permute-start(bf16[160,128]{1,0:T(8,128)(2,1)S(1)} %shard_map.105.a_ref.after_ref), channel_id=1, source_target_pairs={{0,64},{4,68},{8,72},{12,76},{16,80},{20,84},{24,88},{28,92},{64,0... | collective-permute-start | bytes 122888 | tf_op jit(solution)/shard_map/ppermute | solution.py:300
  84.3 19.0 %all-to-all-start.3 = ((bf16[32,32,128]{2,1,0:T(8,128)(2,1)}), bf16[32,32,128]{2,1,0:T(8,128)(2,1)}, u32[]{:S(2)}, u32[]{:S(2)}) async-start(bf16[32,32,128]{2,1,0:T(8,128)(2,1)} %shard_map.107), calls=%async_computation.3 | async-start | bytes 524288 | tf_op jit(solution)/shard_map/all_to_all | solution.py:304
  89.1 9.5 %copy-start = (f32[2048,128]{1,0:T(8,128)S(1)}, f32[2048,128]{1,0:T(8,128)}, u32[]{:S(2)}) copy-start(f32[2048,128]{1,0:T(8,128)} %rows_ref.6) | copy-start | bytes 3145732
  89.1 14.3 %collective-permute-start.1 = (bf16[160,128]{1,0:T(8,128)(2,1)S(1)}, bf16[160,128]{1,0:T(8,128)(2,1)S(1)}, u32[]{:S(2)}, u32[]{:S(2)}) collective-permute-start(bf16[160,128]{1,0:T(8,128)(2,1)S(1)} %shard_map.106.mine_ref), channel_id=1, source_target_pairs={{0,192},{4,196},{8,200},{12,204},{16,208},{20,212},{24,216},{28,22... | collective-permute-start | bytes 122888 | tf_op jit(solution)/shard_map/ppermute | solution.py:300
  123.0 10.2 %collective-permute-start.2 = (bf16[4,384,128]{2,1,0:T(8,128)(2,1)S(1)}, bf16[4,384,128]{2,1,0:T(8,128)(2,1)S(1)}, u32[]{:S(2)}, u32[]{:S(2)}) collective-permute-start(bf16[4,384,128]{2,1,0:T(8,128)(2,1)S(1)} %all_to_all.33.mine_ref), channel_id=1, source_target_pairs={{0,32},{32,0},{1,33},{33,1},{2,34},{34,2},{3,35},{35,3},{4,36},{36... | collective-permute-start | bytes 1179656 | tf_op jit(solution)/shard_map/ppermute | solution.py:363
  130.4 2.8 %copy-start.3 = (f32[1024,128]{1,0:T(8,128)S(1)}, f32[1024,128]{1,0:T(8,128)}, u32[]{:S(2)}) copy-start(f32[1024,128]{1,0:T(8,128)} %rows_ref.7) | copy-start | bytes 1572868
  130.4 2.8 %copy-start.4 = (f32[1024,128]{1,0:T(8,128)S(1)}, f32[1024,128]{1,0:T(8,128)}, u32[]{:S(2)}) copy-start(f32[1024,128]{1,0:T(8,128)} %history_ref.3) | copy-start | bytes 1572868
  133.1 1.3 copy-start.1

commit v6 on v5

--- a/solution.py
+++ b/solution.py
@@ -178,8 +178,7 @@
         part_ref[base : base + BLOCK, :] = part.astype(BF)
 
 
-def serve_kernel(wanted_ref, rows_ref, after_ref, out_ref):
-    del after_ref
+def serve_kernel(wanted_ref, rows_ref, out_ref):
     wanted = wanted_ref[...]
     served = jnp.zeros((OWNERS * CAP, E), F32)
     for base in range(0, RO, BLOCK):
@@ -343,9 +342,9 @@
         [sds((OWNERS, CAP, E), BF)],
         wanted,
         owned_rows,
-        both,
         flops=2 * RO * RO * E,
     )[0]
+    served, both = lax.optimization_barrier((served, both))
     returned = to_owners(served)
     got = far(both, 0)
     both = call(pair_kernel, [sds(both.shape, BF)], both, got, flops=PAIR_COST)[0]

time: 137 us -> 137 us (level)
  blocking collectives: 56.7 us -> 47 us
  starting transfers between devices: 50.6 us -> 56.5 us
  waiting for transfers between devices: 12.1 us -> 15.2 us
    all_to_all x3 -> x2, blocking collectives: 28.6 us -> 18.9 us  [swap(): return lax.all_to_all(x, axes, split_axis=0, concat_axis=0, tiled=True)]
    all_to_all x1 -> x2, waiting for transfers between devices: 9.58 us -> 13.9 us  [swap(): return lax.all_to_all(x, axes, split_axis=0, concat_axis=0, tiled=True)]
    all_to_all x1 -> x2, starting transfers between devices: 17.9 us -> 21.2 us  [swap(): return lax.all_to_all(x, axes, split_axis=0, concat_axis=0, tiled=True)]
    ppermute x2, starting transfers between devices: 20.7 us -> 22.9 us  [far(): return lax.ppermute(x, ('z_hi', 'core', 'z_pair', 'z_odd'), far_pairs(step))]
  transfers between devices with their start and end apart: 5 -> 6, of which waited for: 2 -> 3; matrix products, arithmetic and copies ran while one was open for 0% -> 0% of each run, Pallas kernels for 6% -> 6%
where the time goes in v6:
time: 137 us; the launch traced here: 136 us
  starting transfers between devices  56.5 us (41%)
  blocking collectives  47 us (34%)
  Pallas kernels  16.6 us (12%)
  waiting for transfers between devices  15.2 us (11%)
    all_to_all x1, blocking collectives, to_owners(): lax.all_to_all(x, ('z_hi', 'core', 'z_pair', 'z_odd', 'y'), split_axis=0,...  28.1 us
    ppermute x2, starting transfers between devices, far(): return lax.ppermute(x, ('z_hi', 'core', 'z_pair', 'z_odd'), far_pairs(step))  22.9 us
    all_to_all x2, starting transfers between devices, swap(): return lax.all_to_all(x, axes, split_axis=0, concat_axis=0, tiled=True)  21.2 us
    all_to_all x2, blocking collectives, swap(): return lax.all_to_all(x, axes, split_axis=0, concat_axis=0, tiled=True)  18.9 us
    all_to_all x2, waiting for transfers between devices, swap(): return lax.all_to_all(x, axes, split_axis=0, concat_axis=0, tiled=True)  13.9 us
    pallas_call x12, Pallas kernels, call(): pl.pallas_call(kernel, out_shape=outs, in_specs=[pl.BlockSpec(memory_spac...  13 us
    ppermute x1, starting transfers between devices, body(): other = lax.ppermute(mine, 'core', [(0, 1), (1, 0)])  7.73 us
    all_to_all x1, starting transfers between devices, to_owners(): lax.all_to_all(x, ('z_hi', 'core', 'z_pair', 'z_odd', 'y'), split_axis=0,...  4.7 us
  transfers between devices with their start and end apart: 6, of which 3 were waited for; matrix products, arithmetic and copies ran while one was open for 0% of the time, Pallas kernels for 6%

profile of v6, /device:TPU:1, one launch (start us, length us, event | category | flops | bytes accessed | tf_op | source)
XLA Modules:
  0.0 136.2 jit_solution(7940288946913367782)
XLA Ops:
  0.6 3.6 %shard_map.102 = bf16[2048,128]{1,0:T(8,128)(2,1)} custom-call(s32[32,128]{1,0:T(8,128)} %bitcast.5, bf16[128,1024]{1,0:T(8,128)(2,1)} %grad_hbm.1), custom_call_target="tpu_custom_call" | custom-call | tf_op jit(solution)/shard_map/pallas_call | solution.py:82
  4.3 0.0 copy-start.5
  4.3 0.0 copy-start.6
  4.3 17.9 %all-to-all-start = ((bf16[32,64,128]{2,1,0:T(8,128)(2,1)}), bf16[32,64,128]{2,1,0:T(8,128)(2,1)S(1)}, u32[]{:S(2)}, u32[]{:S(2)}) async-start(bf16[32,64,128]{2,1,0:T(8,128)(2,1)} %bitcast.8), calls=%async_computation | async-start | bytes 1048576 | tf_op jit(solution)/shard_map/all_to_all | solution.py:264
  22.2 1.5 %shard_map.101 = (bf16[32,32,128]{2,1,0:T(8,128)(2,1)S(1)}, f32[64,128]{1,0:T(8,128)S(1)}, s32[32,128]{1,0:T(8,128)S(1)}) custom-call(s32[32,128]{1,0:T(8,128)S(1)} %bitcast.6, bf16[128,1024]{1,0:T(8,128)(2,1)S(1)} %copy-done.5), custom_call_target="tpu_custom_call" | custom-call | flops 268435456 | bytes 589824 | tf_op jit(solution)/shard_map/pallas_call | solution.py:30
  23.7 9.6 %all-to-all-done.got_ref = bf16[32,64,128]{2,1,0:T(8,128)(2,1)S(1)} async-done(((bf16[32,64,128]{2,1,0:T(8,128)(2,1)}), bf16[32,64,128]{2,1,0:T(8,128)(2,1)S(1)}, u32[]{:S(2)}, u32[]{:S(2)}) %all-to-all-start) | async-done | bytes 524320 | tf_op jit(solution)/shard_map/all_to_all | solution.py:264
  33.3 0.1 shard_map.103
  33.4 28.1 %all_to_all.30.got_ref = bf16[32,42,128]{2,1,0:T(8,128)(2,1)S(1)} all-to-all(bf16[32,42,128]{2,1,0:T(8,128)(2,1)S(1)} %shard_map.103), channel_id=1, replica_groups={{0,1,2,3,4,5,6,7,8,9,10,11,12,13,14,15,16,17,18,19,20,21,22,23,24,25,26..., dimensions={0} | all-to-all | bytes 688128 | tf_op jit(solution)/shard_map/all_to_all | solution.py:303
  61.5 1.6 %shard_map.104 = (bf16[1024,128]{1,0:T(8,128)(2,1)}, s32[8,128]{1,0:T(8,128)S(1)}, bf16[32,128]{1,0:T(8,128)(2,1)S(1)}) custom-call(bf16[32,42,128]{2,1,0:T(8,128)(2,1)S(1)} %all_to_all.30.got_ref), custom_call_target="tpu_custom_call" | custom-call | flops 268435456 | bytes 618496 | tf_op jit(solution)/shard_map/pallas_call | solution.py:30
  63.1 3.4 %all-to-all-start.2 = ((bf16[8,128,128]{2,1,0:T(8,128)(2,1)}), bf16[8,128,128]{2,1,0:T(8,128)(2,1)S(1)}, u32[]{:S(2)}, u32[]{:S(2)}) async-start(bf16[8,128,128]{2,1,0:T(8,128)(2,1)} %bitcast.2), calls=%async_computation.2 | async-start | bytes 524288 | tf_op jit(solution)/shard_map/all_to_all | solution.py:264
  66.5 1.5 %shard_map.105 = bf16[32,32,128]{2,1,0:T(8,128)(2,1)} custom-call(s32[8,128]{1,0:T(8,128)S(1)} %get-tuple-element.24.wanted_ref, f32[1024,128]{1,0:T(8,128)S(1)} %copy-done.2), custom_call_target="tpu_custom_call" | custom-call | flops 268435456 | bytes 790528 | tf_op jit(solution)/shard_map/pallas_call | solution.py:30
  68.0 4.3 %all-to-all-done.2.got_ref = bf16[8,128,128]{2,1,0:T(8,128)(2,1)S(1)} async-done(((bf16[8,128,128]{2,1,0:T(8,128)(2,1)}), bf16[8,128,128]{2,1,0:T(8,128)(2,1)S(1)}, u32[]{:S(2)}, u32[]{:S(2)}) %all-to-all-start.2) | async-done | bytes 262176 | tf_op jit(solution)/shard_map/all_to_all | solution.py:264
  72.3 12.0 %collective-permute-start = (bf16[160,128]{1,0:T(8,128)(2,1)S(1)}, bf16[160,128]{1,0:T(8,128)(2,1)S(1)}, u32[]{:S(2)}, u32[]{:S(2)}) collective-permute-start(bf16[160,128]{1,0:T(8,128)(2,1)S(1)} %shard_map.106.a_ref), channel_id=1, source_target_pairs={{0,64},{4,68},{8,72},{12,76},{16,80},{20,84},{24,88},{28,92},{64,0... | collective-permute-start | bytes 122888 | tf_op jit(solution)/shard_map/ppermute | solution.py:299
  84.4 4.7 %all-to-all-start.3 = ((bf16[32,32,128]{2,1,0:T(8,128)(2,1)}), bf16[32,32,128]{2,1,0:T(8,128)(2,1)}, u32[]{:S(2)}, u32[]{:S(2)}) async-start(bf16[32,32,128]{2,1,0:T(8,128)(2,1)} %shard_map.105), calls=%async_computation.3 | async-start | bytes 524288 | tf_op jit(solution)/shard_map/all_to_all | solution.py:303
  89.1 0.0 collective-permute-done.b_ref
  89.1 0.0 copy-start
  89.1 10.9 %collective-permute-start.1 = (bf16[160,128]{1,0:T(8,128)(2,1)S(1)}, bf16[160,128]{1,0:T(8,128)(2,1)S(1)}, u32[]{:S(2)}, u32[]{:S(2)}) collective-permute-start(bf16[160,128]{1,0:T(8,128)(2,1)S(1)} %shard_map.107.mine_ref), channel_id=1, source_target_pairs={{0,192},{4,196},{8,200},{12,204},{16,208},{20,212},{24,216},{28,22... | collective-permute-start | bytes 122888 | tf_op jit(solution)/shard_map/ppermute | solution.py:299
  100.0 0.0 copy-done
  100.0 2.3 %shard_map.108.part_ref.after_ref = f32[1024,128]{1,0:T(8,128)S(1)} custom-call(s32[32,128]{1,0:T(8,128)S(1)} %bitcast.7, f32[2048,128]{1,0:T(8,128)S(1)} %copy-done), custom_call_target="tpu_custom_call" | custom-call | flops 536870912 | bytes 1589248 | tf_op jit(solution)/shard_map/pallas_call | solution.py:30
  102.3 1.3 collective-permute-done.1.got_ref
  103.6 0.0 all-to-all-done.3
  103.7 10.2 %all_to_all.31.got_ref = bf16[8,32,128]{2,1,0:T(8,128)(2,1)S(1)} all-to-all(bf16[8,32,128]{2,1,0:T(8,128)(2,1)S(1)} %get-tuple-element.31), channel_id=1, replica_groups=mesh['x'=4,'z_hi'=4,'core'=2,'z_pair'=4,'z_odd'=2,'y'=4] {'z_odd','y'}, dimensions={0} | all-to-all | bytes 131072 | tf_op jit(solution)/shard_map/all_to_all | solution.py:264
  113.9 0.1 shard_map.111
  113.9 8.6 %all_to_all.32.mine_ref = bf16[4,384,128]{2,1,0:T(8,128)(2,1)S(1)} all-to-all(bf16[4,384,128]{2,1,0:T(8,128)(2,1)S(1)} %shard_map.111), channel_id=1, replica_groups=mesh['x'=4,'z_hi'=4,'core'=2,'z_pair'=4,'z_odd'=2,'y'=4] {'x'}, dimensions={0} | all-to-all | bytes 786432 | tf_op jit(solution)/shard_map/all_to_all | solution.py:264
  122.6 7.7 %collective-permute-start.2 = (bf16[4,384,128]{2,1,0:T(8,128)(2,1)S(1)}, bf16[4,384,128]{2,1,0:T(8,128)(2,1)S(1)}, u32[]{:S(2)}, u32[]{:S(2)}) collective-permute-start(bf16[4,384,128]{2,1,0:T(8,128)(2,1)S(1)} %all_to_all.32.mine_ref), channel_id=1, source_target_pairs={{0,32},{32,0},{1,33},{33,1},{2,34},{34,2},{3,35},{35,3},{4,36},{36... | collective-permute-start | bytes 1179656 | tf_op jit(solution)/shard_map/ppermute | solution.py:362
  130.3 0.0 copy-start.3
  130.3 0.0 copy-start.4
  130.3 2.7 %shard_map.109 = bf16[128,1024]{1,0:T(8,128)(2,1)} custom-call(s32[32,128]{1,0:T(8,128)S(1)} %get-tuple-element.21.slot_ref, bf16[1024,128]{1,0:T(8,128)(2,1)} %bitcast.3.rows_ref, f32[1024,128]{1,0:T(8,128)S(1)} %shard_map.108.part_ref.after_ref), custom_call_target="tpu_custom_call" | custom-call | flops 268435456 | bytes 1064960 | tf_op jit(solution)/shard_map/pallas_call | solution.py:30
  133.1 0.0 collective-permute-done.2.other_ref
  133.1 0.0 copy-done.3
  133.1 1.2 shard_map.113
  134.3 1.8 %shard_map.112 = (f32[2048,128]{1,0:T(8,128)}, f32[2048,128]{1,0:T(8,128)}) custom-call(s32[1]{0:T(128)} %bitcast.4.core_ref, bf16[4,384,128]{2,1,0:T(8,128)(2,1)S(1)} %all_to_all.32.mine_ref, bf16[4,384,128]{2,1,0:T(8,128)(2,1)S(1)} %collective-permute-done.2.other_ref, f32[2048,128]{1,0:T(8,128)S(1)} %copy-done, f32[2048,128]{1,0:T(8,128)S(1)} %copy-done.1), custom_call_target="tpu_custom_call" | custom-call | bytes 4980740 | tf_op jit(solution)/shard_map/pallas_call | solution.py:30
  (10 shorter events, 0.1 us)
Async XLA Ops:
  4.3 17.9 %copy-start.5 = (bf16[128,1024]{1,0:T(8,128)(2,1)S(1)}, bf16[128,1024]{1,0:T(8,128)(2,1)}, u32[]{:S(2)}) copy-start(bf16[128,1024]{1,0:T(8,128)(2,1)} %grad_hbm.1) | copy-start | bytes 786436
  4.3 17.9 %copy-start.6 = (s32[128,32]{0,1:T(8,128)S(1)}, s32[128,32]{0,1:T(8,128)}, u32[]{:S(2)}) copy-start(s32[128,32]{0,1:T(8,128)} %param.6) | copy-start | bytes 49156
  4.3 29.0 %all-to-all-start = ((bf16[32,64,128]{2,1,0:T(8,128)(2,1)}), bf16[32,64,128]{2,1,0:T(8,128)(2,1)S(1)}, u32[]{:S(2)}, u32[]{:S(2)}) async-start(bf16[32,64,128]{2,1,0:T(8,128)(2,1)} %bitcast.8), calls=%async_computation | async-start | bytes 1048576 | tf_op jit(solution)/shard_map/all_to_all | solution.py:264
  61.5 5.0 %copy-start.2 = (f32[1024,128]{1,0:T(8,128)S(1)}, f32[1024,128]{1,0:T(8,128)}, u32[]{:S(2)}) copy-start(f32[1024,128]{1,0:T(8,128)} %rows_ref.7) | copy-start | bytes 1572868
  63.1 9.2 %all-to-all-start.2 = ((bf16[8,128,128]{2,1,0:T(8,128)(2,1)}), bf16[8,128,128]{2,1,0:T(8,128)(2,1)S(1)}, u32[]{:S(2)}, u32[]{:S(2)}) async-start(bf16[8,128,128]{2,1,0:T(8,128)(2,1)} %bitcast.2), calls=%async_computation.2 | async-start | bytes 524288 | tf_op jit(solution)/shard_map/all_to_all | solution.py:264
  72.3 16.7 %collective-permute-start = (bf16[160,128]{1,0:T(8,128)(2,1)S(1)}, bf16[160,128]{1,0:T(8,128)(2,1)S(1)}, u32[]{:S(2)}, u32[]{:S(2)}) collective-permute-start(bf16[160,128]{1,0:T(8,128)(2,1)S(1)} %shard_map.106.a_ref), channel_id=1, source_target_pairs={{0,64},{4,68},{8,72},{12,76},{16,80},{20,84},{24,88},{28,92},{64,0... | collective-permute-start | bytes 122888 | tf_op jit(solution)/shard_map/ppermute | solution.py:299
  84.4 19.3 %all-to-all-start.3 = ((bf16[32,32,128]{2,1,0:T(8,128)(2,1)}), bf16[32,32,128]{2,1,0:T(8,128)(2,1)}, u32[]{:S(2)}, u32[]{:S(2)}) async-start(bf16[32,32,128]{2,1,0:T(8,128)(2,1)} %shard_map.105), calls=%async_computation.3 | async-start | bytes 524288 | tf_op jit(solution)/shard_map/all_to_all | solution.py:303
  89.1 10.9 %copy-start = (f32[2048,128]{1,0:T(8,128)S(1)}, f32[2048,128]{1,0:T(8,128)}, u32[]{:S(2)}) copy-start(f32[2048,128]{1,0:T(8,128)} %rows_ref.6) | copy-start | bytes 3145732
  89.1 14.5 %collective-permute-start.1 = (bf16[160,128]{1,0:T(8,128)(2,1)S(1)}, bf16[160,128]{1,0:T(8,128)(2,1)S(1)}, u32[]{:S(2)}, u32[]{:S(2)}) collective-permute-start(bf16[160,128]{1,0:T(8,128)(2,1)S(1)} %shard_map.107.mine_ref), channel_id=1, source_target_pairs={{0,192},{4,196},{8,200},{12,204},{16,208},{20,212},{24,216},{28,22... | collective-permute-start | bytes 122888 | tf_op jit(solution)/shard_map/ppermute | solution.py:299
  122.6 10.5 %collective-permute-start.2 = (bf16[4,384,128]{2,1,0:T(8,128)(2,1)S(1)}, bf16[4,384,128]{2,1,0:T(8,128)(2,1)S(1)}, u32[]{:S(2)}, u32[]{:S(2)}) collective-permute-start(bf16[4,384,128]{2,1,0:T(8,128)(2,1)S(1)} %all_to_all.32.mine_ref), channel_id=1, source_target_pairs={{0,32},{32,0},{1,33},{33,1},{2,34},{34,2},{3,35},{35,3},{4,36},{36... | collective-permute-start | bytes 1179656 | tf_op jit(solution)/shard_map/ppermute | solution.py:362
  130.3 2.8 %copy-start.3 = (f32[1024,128]{1,0:T(8,128)S(1)}, f32[1024,128]{1,0:T(8,128)}, u32[]{:S(2)}) copy-start(f32[1024,128]{1,0:T(8,128)} %rows_ref.7) | copy-start | bytes 1572868
  130.3 2.8 %copy-start.4 = (f32[1024,128]{1,0:T(8,128)S(1)}, f32[1024,128]{1,0:T(8,128)}, u32[]{:S(2)}) copy-start(f32[1024,128]{1,0:T(8,128)} %history_ref.3) | copy-start | bytes 1572868
  133.1 1.3 copy-start.1

commit v7 on v6

--- a/solution.py
+++ b/solution.py
@@ -62,18 +62,20 @@
     return jnp.concatenate([grad[:, f * E : (f + 1) * E] for f in range(F)], axis=0)
 
 
-def frequent_kernel(index_hbm, grad_hbm, part_ref, index_ref, grad_ref, sems):
+def frequent_kernel(index_hbm, grad_hbm, part_ref, index_ref, grad_ref, hits_ref, sems):
     index_copy = pltpu.make_async_copy(index_hbm, index_ref, sems.at[0])
     grad_copy = pltpu.make_async_copy(grad_hbm, grad_ref, sems.at[1])
     index_copy.start()
     grad_copy.start()
     index_copy.wait()
     index = index_ref[...]
-    first = counts(index, 0)
+    early = hits_ref.shape[0]
+    for base in range(0, early, BLOCK):
+        hits_ref[base : base + BLOCK, :] = counts(index, base)
     grad_copy.wait()
     grad = stack_tables(grad_ref[...])
     for base in range(0, NF, BLOCK):
-        hits = counts(index, base) if base else first
+        hits = hits_ref[base : base + BLOCK, :] if base < early else counts(index, base)
         part = jnp.dot(hits, grad, preferred_element_type=F32)
         part_ref[base : base + BLOCK, :] = part.astype(BF)
 
@@ -87,6 +89,7 @@
         scratch_shapes=[
             pltpu.VMEM(index.shape, index.dtype),
             pltpu.VMEM(grad.shape, grad.dtype),
+            pltpu.VMEM((NF // 2, F * B), BF),
             pltpu.SemaphoreType.DMA((2,)),
         ],
         compiler_params=pltpu.CompilerParams(vmem_limit_bytes=60 * 1024 * 1024),
@@ -245,7 +248,7 @@
 def adagrad(rows, history, grad):
     grad = grad.astype(F32)
     new = history + grad * grad
-    return rows - 0.5 * grad / jnp.sqrt(new + 1e-08), new
+    return rows - 0.5 * grad * lax.rsqrt(new + 1e-08), new
 
 
 def adagrad_kernel(core_ref, mine_ref, other_ref, rows_ref, history_ref, updated_ref, new_ref):

time: 137 us -> 137 us (level)
  no operation moved by 1% of the time
where the time goes in v7:
time: 137 us; the launch traced here: 136 us
  starting transfers between devices  56.5 us (41%)
  blocking collectives  46.9 us (34%)
  Pallas kernels  16.5 us (12%)
  waiting for transfers between devices  15.2 us (11%)
    all_to_all x1, blocking collectives, to_owners(): lax.all_to_all(x, ('z_hi', 'core', 'z_pair', 'z_odd', 'y'), split_axis=0,...  28.1 us
    ppermute x2, starting transfers between devices, far(): return lax.ppermute(x, ('z_hi', 'core', 'z_pair', 'z_odd'), far_pairs(step))  22.9 us
    all_to_all x2, starting transfers between devices, swap(): return lax.all_to_all(x, axes, split_axis=0, concat_axis=0, tiled=True)  21.2 us
    all_to_all x2, blocking collectives, swap(): return lax.all_to_all(x, axes, split_axis=0, concat_axis=0, tiled=True)  18.8 us
    all_to_all x2, waiting for transfers between devices, swap(): return lax.all_to_all(x, axes, split_axis=0, concat_axis=0, tiled=True)  13.9 us
    pallas_call x12, Pallas kernels, call(): pl.pallas_call(kernel, out_shape=outs, in_specs=[pl.BlockSpec(memory_spac...  12.6 us
    ppermute x1, starting transfers between devices, body(): other = lax.ppermute(mine, 'core', [(0, 1), (1, 0)])  7.74 us
    all_to_all x1, starting transfers between devices, to_owners(): lax.all_to_all(x, ('z_hi', 'core', 'z_pair', 'z_odd', 'y'), split_axis=0,...  4.7 us
  transfers between devices with their start and end apart: 6, of which 3 were waited for; matrix products, arithmetic and copies ran while one was open for 0% of the time, Pallas kernels for 6%

profile of v7, /device:TPU:1, one launch (start us, length us, event | category | flops | bytes accessed | tf_op | source)
XLA Modules:
  0.0 136.5 jit_solution(13053253622858497236)
XLA Ops:
  0.6 3.9 %shard_map.102 = bf16[2048,128]{1,0:T(8,128)(2,1)} custom-call(s32[32,128]{1,0:T(8,128)} %bitcast.5, bf16[128,1024]{1,0:T(8,128)(2,1)} %grad_hbm.1), custom_call_target="tpu_custom_call" | custom-call | tf_op jit(solution)/shard_map/pallas_call | solution.py:84
  4.5 0.0 copy-start.5
  4.5 0.0 copy-start.6
  4.5 17.9 %all-to-all-start = ((bf16[32,64,128]{2,1,0:T(8,128)(2,1)}), bf16[32,64,128]{2,1,0:T(8,128)(2,1)S(1)}, u32[]{:S(2)}, u32[]{:S(2)}) async-start(bf16[32,64,128]{2,1,0:T(8,128)(2,1)} %bitcast.8), calls=%async_computation | async-start | bytes 1048576 | tf_op jit(solution)/shard_map/all_to_all | solution.py:267
  22.4 0.0 copy-done.5
  22.4 1.5 %shard_map.101 = (bf16[32,32,128]{2,1,0:T(8,128)(2,1)S(1)}, f32[64,128]{1,0:T(8,128)S(1)}, s32[32,128]{1,0:T(8,128)S(1)}) custom-call(s32[32,128]{1,0:T(8,128)S(1)} %bitcast.6, bf16[128,1024]{1,0:T(8,128)(2,1)S(1)} %copy-done.5), custom_call_target="tpu_custom_call" | custom-call | flops 268435456 | bytes 589824 | tf_op jit(solution)/shard_map/pallas_call | solution.py:30
  23.9 9.6 %all-to-all-done.got_ref = bf16[32,64,128]{2,1,0:T(8,128)(2,1)S(1)} async-done(((bf16[32,64,128]{2,1,0:T(8,128)(2,1)}), bf16[32,64,128]{2,1,0:T(8,128)(2,1)S(1)}, u32[]{:S(2)}, u32[]{:S(2)}) %all-to-all-start) | async-done | bytes 524320 | tf_op jit(solution)/shard_map/all_to_all | solution.py:267
  33.5 0.1 shard_map.103
  33.7 28.1 %all_to_all.30.got_ref = bf16[32,42,128]{2,1,0:T(8,128)(2,1)S(1)} all-to-all(bf16[32,42,128]{2,1,0:T(8,128)(2,1)S(1)} %shard_map.103), channel_id=1, replica_groups={{0,1,2,3,4,5,6,7,8,9,10,11,12,13,14,15,16,17,18,19,20,21,22,23,24,25,26..., dimensions={0} | all-to-all | bytes 688128 | tf_op jit(solution)/shard_map/all_to_all | solution.py:306
  61.8 1.6 %shard_map.104 = (bf16[1024,128]{1,0:T(8,128)(2,1)}, s32[8,128]{1,0:T(8,128)S(1)}, bf16[32,128]{1,0:T(8,128)(2,1)S(1)}) custom-call(bf16[32,42,128]{2,1,0:T(8,128)(2,1)S(1)} %all_to_all.30.got_ref), custom_call_target="tpu_custom_call" | custom-call | flops 268435456 | bytes 618496 | tf_op jit(solution)/shard_map/pallas_call | solution.py:30
  63.4 3.4 %all-to-all-start.2 = ((bf16[8,128,128]{2,1,0:T(8,128)(2,1)}), bf16[8,128,128]{2,1,0:T(8,128)(2,1)S(1)}, u32[]{:S(2)}, u32[]{:S(2)}) async-start(bf16[8,128,128]{2,1,0:T(8,128)(2,1)} %bitcast.2), calls=%async_computation.2 | async-start | bytes 524288 | tf_op jit(solution)/shard_map/all_to_all | solution.py:267
  66.7 1.5 %shard_map.105 = bf16[32,32,128]{2,1,0:T(8,128)(2,1)} custom-call(s32[8,128]{1,0:T(8,128)S(1)} %get-tuple-element.24.wanted_ref, f32[1024,128]{1,0:T(8,128)S(1)} %copy-done.2), custom_call_target="tpu_custom_call" | custom-call | flops 268435456 | bytes 790528 | tf_op jit(solution)/shard_map/pallas_call | solution.py:30
  68.2 4.3 %all-to-all-done.2.got_ref = bf16[8,128,128]{2,1,0:T(8,128)(2,1)S(1)} async-done(((bf16[8,128,128]{2,1,0:T(8,128)(2,1)}), bf16[8,128,128]{2,1,0:T(8,128)(2,1)S(1)}, u32[]{:S(2)}, u32[]{:S(2)}) %all-to-all-start.2) | async-done | bytes 262176 | tf_op jit(solution)/shard_map/all_to_all | solution.py:267
  72.6 12.0 %collective-permute-start = (bf16[160,128]{1,0:T(8,128)(2,1)S(1)}, bf16[160,128]{1,0:T(8,128)(2,1)S(1)}, u32[]{:S(2)}, u32[]{:S(2)}) collective-permute-start(bf16[160,128]{1,0:T(8,128)(2,1)S(1)} %shard_map.106.a_ref), channel_id=1, source_target_pairs={{0,64},{4,68},{8,72},{12,76},{16,80},{20,84},{24,88},{28,92},{64,0... | collective-permute-start | bytes 122888 | tf_op jit(solution)/shard_map/ppermute | solution.py:302
  84.6 4.7 %all-to-all-start.3 = ((bf16[32,32,128]{2,1,0:T(8,128)(2,1)}), bf16[32,32,128]{2,1,0:T(8,128)(2,1)}, u32[]{:S(2)}, u32[]{:S(2)}) async-start(bf16[32,32,128]{2,1,0:T(8,128)(2,1)} %shard_map.105), calls=%async_computation.3 | async-start | bytes 524288 | tf_op jit(solution)/shard_map/all_to_all | solution.py:306
  89.3 0.0 collective-permute-done.b_ref
  89.3 0.0 copy-start
  89.3 10.9 %collective-permute-start.1 = (bf16[160,128]{1,0:T(8,128)(2,1)S(1)}, bf16[160,128]{1,0:T(8,128)(2,1)S(1)}, u32[]{:S(2)}, u32[]{:S(2)}) collective-permute-start(bf16[160,128]{1,0:T(8,128)(2,1)S(1)} %shard_map.107.mine_ref), channel_id=1, source_target_pairs={{0,192},{4,196},{8,200},{12,204},{16,208},{20,212},{24,216},{28,22... | collective-permute-start | bytes 122888 | tf_op jit(solution)/shard_map/ppermute | solution.py:302
  100.2 2.3 %shard_map.108.part_ref.after_ref = f32[1024,128]{1,0:T(8,128)S(1)} custom-call(s32[32,128]{1,0:T(8,128)S(1)} %bitcast.7, f32[2048,128]{1,0:T(8,128)S(1)} %copy-done), custom_call_target="tpu_custom_call" | custom-call | flops 536870912 | bytes 1589248 | tf_op jit(solution)/shard_map/pallas_call | solution.py:30
  102.6 1.3 collective-permute-done.1.got_ref
  103.9 0.0 all-to-all-done.3
  103.9 10.2 %all_to_all.31.got_ref = bf16[8,32,128]{2,1,0:T(8,128)(2,1)S(1)} all-to-all(bf16[8,32,128]{2,1,0:T(8,128)(2,1)S(1)} %get-tuple-element.31), channel_id=1, replica_groups=mesh['x'=4,'z_hi'=4,'core'=2,'z_pair'=4,'z_odd'=2,'y'=4] {'z_odd','y'}, dimensions={0} | all-to-all | bytes 131072 | tf_op jit(solution)/shard_map/all_to_all | solution.py:267
  114.1 0.1 shard_map.111
  114.2 8.6 %all_to_all.32.mine_ref = bf16[4,384,128]{2,1,0:T(8,128)(2,1)S(1)} all-to-all(bf16[4,384,128]{2,1,0:T(8,128)(2,1)S(1)} %shard_map.111), channel_id=1, replica_groups=mesh['x'=4,'z_hi'=4,'core'=2,'z_pair'=4,'z_odd'=2,'y'=4] {'x'}, dimensions={0} | all-to-all | bytes 786432 | tf_op jit(solution)/shard_map/all_to_all | solution.py:267
  122.8 7.7 %collective-permute-start.2 = (bf16[4,384,128]{2,1,0:T(8,128)(2,1)S(1)}, bf16[4,384,128]{2,1,0:T(8,128)(2,1)S(1)}, u32[]{:S(2)}, u32[]{:S(2)}) collective-permute-start(bf16[4,384,128]{2,1,0:T(8,128)(2,1)S(1)} %all_to_all.32.mine_ref), channel_id=1, source_target_pairs={{0,32},{32,0},{1,33},{33,1},{2,34},{34,2},{3,35},{35,3},{4,36},{36... | collective-permute-start | bytes 1179656 | tf_op jit(solution)/shard_map/ppermute | solution.py:365
  130.5 0.0 copy-start.3
  130.6 0.0 copy-start.4
  130.6 2.7 %shard_map.109 = bf16[128,1024]{1,0:T(8,128)(2,1)} custom-call(s32[32,128]{1,0:T(8,128)S(1)} %get-tuple-element.21.slot_ref, bf16[1024,128]{1,0:T(8,128)(2,1)} %bitcast.3.rows_ref, f32[1024,128]{1,0:T(8,128)S(1)} %shard_map.108.part_ref.after_ref), custom_call_target="tpu_custom_call" | custom-call | flops 268435456 | bytes 1064960 | tf_op jit(solution)/shard_map/pallas_call | solution.py:30
  133.3 0.0 collective-permute-done.2.other_ref
  133.3 1.1 shard_map.113
  134.4 0.5 copy-done.1
  134.9 1.6 %shard_map.112 = (f32[2048,128]{1,0:T(8,128)}, f32[2048,128]{1,0:T(8,128)}) custom-call(s32[1]{0:T(128)} %bitcast.4.core_ref, bf16[4,384,128]{2,1,0:T(8,128)(2,1)S(1)} %all_to_all.32.mine_ref, bf16[4,384,128]{2,1,0:T(8,128)(2,1)S(1)} %collective-permute-done.2.other_ref, f32[2048,128]{1,0:T(8,128)S(1)} %copy-done, f32[2048,128]{1,0:T(8,128)S(1)} %copy-done.1), custom_call_target="tpu_custom_call" | custom-call | bytes 4980740 | tf_op jit(solution)/shard_map/pallas_call | solution.py:30
  (10 shorter events, 0.1 us)
Async XLA Ops:
  4.5 17.9 %copy-start.5 = (bf16[128,1024]{1,0:T(8,128)(2,1)S(1)}, bf16[128,1024]{1,0:T(8,128)(2,1)}, u32[]{:S(2)}) copy-start(bf16[128,1024]{1,0:T(8,128)(2,1)} %grad_hbm.1) | copy-start | bytes 786436
  4.5 17.9 %copy-start.6 = (s32[128,32]{0,1:T(8,128)S(1)}, s32[128,32]{0,1:T(8,128)}, u32[]{:S(2)}) copy-start(s32[128,32]{0,1:T(8,128)} %param.6) | copy-start | bytes 49156
  4.5 29.0 %all-to-all-start = ((bf16[32,64,128]{2,1,0:T(8,128)(2,1)}), bf16[32,64,128]{2,1,0:T(8,128)(2,1)S(1)}, u32[]{:S(2)}, u32[]{:S(2)}) async-start(bf16[32,64,128]{2,1,0:T(8,128)(2,1)} %bitcast.8), calls=%async_computation | async-start | bytes 1048576 | tf_op jit(solution)/shard_map/all_to_all | solution.py:267
  61.8 5.0 %copy-start.2 = (f32[1024,128]{1,0:T(8,128)S(1)}, f32[1024,128]{1,0:T(8,128)}, u32[]{:S(2)}) copy-start(f32[1024,128]{1,0:T(8,128)} %rows_ref.7) | copy-start | bytes 1572868
  63.4 9.2 %all-to-all-start.2 = ((bf16[8,128,128]{2,1,0:T(8,128)(2,1)}), bf16[8,128,128]{2,1,0:T(8,128)(2,1)S(1)}, u32[]{:S(2)}, u32[]{:S(2)}) async-start(bf16[8,128,128]{2,1,0:T(8,128)(2,1)} %bitcast.2), calls=%async_computation.2 | async-start | bytes 524288 | tf_op jit(solution)/shard_map/all_to_all | solution.py:267
  72.6 16.7 %collective-permute-start = (bf16[160,128]{1,0:T(8,128)(2,1)S(1)}, bf16[160,128]{1,0:T(8,128)(2,1)S(1)}, u32[]{:S(2)}, u32[]{:S(2)}) collective-permute-start(bf16[160,128]{1,0:T(8,128)(2,1)S(1)} %shard_map.106.a_ref), channel_id=1, source_target_pairs={{0,64},{4,68},{8,72},{12,76},{16,80},{20,84},{24,88},{28,92},{64,0... | collective-permute-start | bytes 122888 | tf_op jit(solution)/shard_map/ppermute | solution.py:302
  84.6 19.3 %all-to-all-start.3 = ((bf16[32,32,128]{2,1,0:T(8,128)(2,1)}), bf16[32,32,128]{2,1,0:T(8,128)(2,1)}, u32[]{:S(2)}, u32[]{:S(2)}) async-start(bf16[32,32,128]{2,1,0:T(8,128)(2,1)} %shard_map.105), calls=%async_computation.3 | async-start | bytes 524288 | tf_op jit(solution)/shard_map/all_to_all | solution.py:306
  89.3 10.9 %copy-start = (f32[2048,128]{1,0:T(8,128)S(1)}, f32[2048,128]{1,0:T(8,128)}, u32[]{:S(2)}) copy-start(f32[2048,128]{1,0:T(8,128)} %rows_ref.6) | copy-start | bytes 3145732
  89.3 14.5 %collective-permute-start.1 = (bf16[160,128]{1,0:T(8,128)(2,1)S(1)}, bf16[160,128]{1,0:T(8,128)(2,1)S(1)}, u32[]{:S(2)}, u32[]{:S(2)}) collective-permute-start(bf16[160,128]{1,0:T(8,128)(2,1)S(1)} %shard_map.107.mine_ref), channel_id=1, source_target_pairs={{0,192},{4,196},{8,200},{12,204},{16,208},{20,212},{24,216},{28,22... | collective-permute-start | bytes 122888 | tf_op jit(solution)/shard_map/ppermute | solution.py:302
  122.8 10.5 %collective-permute-start.2 = (bf16[4,384,128]{2,1,0:T(8,128)(2,1)S(1)}, bf16[4,384,128]{2,1,0:T(8,128)(2,1)S(1)}, u32[]{:S(2)}, u32[]{:S(2)}) collective-permute-start(bf16[4,384,128]{2,1,0:T(8,128)(2,1)S(1)} %all_to_all.32.mine_ref), channel_id=1, source_target_pairs={{0,32},{32,0},{1,33},{33,1},{2,34},{34,2},{3,35},{35,3},{4,36},{36... | collective-permute-start | bytes 1179656 | tf_op jit(solution)/shard_map/ppermute | solution.py:365
  130.5 2.8 %copy-start.3 = (f32[1024,128]{1,0:T(8,128)S(1)}, f32[1024,128]{1,0:T(8,128)}, u32[]{:S(2)}) copy-start(f32[1024,128]{1,0:T(8,128)} %rows_ref.7) | copy-start | bytes 1572868
  130.6 2.8 %copy-start.4 = (f32[1024,128]{1,0:T(8,128)S(1)}, f32[1024,128]{1,0:T(8,128)}, u32[]{:S(2)}) copy-start(f32[1024,128]{1,0:T(8,128)} %history_ref.3) | copy-start | bytes 1572868
  133.3 1.6 %copy-start.1 = (f32[2048,128]{1,0:T(8,128)S(1)}, f32[2048,128]{1,0:T(8,128)}, u32[]{:S(2)}) copy-start(f32[2048,128]{1,0:T(8,128)} %history_ref.2) | copy-start | bytes 3145732
